TPU v7x, 256 devices: a whole 4x4x8 slice. The times are simulated.
256 devices in a mesh: branch: 4 (over y), seq: 16 (over z_lo, x, core), mp: 4 (over z_hi).
Axes of the slice: x: 4, y: 4, z: 8 (z_hi: 4, z_lo: 2; z = z_hi * 2 + z_lo), core: 2. Of those that a mesh axis runs over, the one named last changes fastest.
Arguments:
- span_q: bfloat16 [4, 2048, 2560], P('branch', 'seq', 'mp'), may hold values from -6 to 6
- span_k: bfloat16 [4, 2048, 2560], P('branch', 'seq', 'mp'), may hold values from -6 to 6
- span_v: bfloat16 [4, 2048, 2560], P('branch', 'seq', 'mp'), may hold values from -6 to 6
- hist_k: bfloat16 [4, 8192, 2560], P('branch', 'seq', 'mp'), may hold values from -6 to 6
- hist_v: bfloat16 [4, 8192, 2560], P('branch', 'seq', 'mp'), may hold values from -6 to 6
- hist_len: int32 [4], replicated, may hold values from 0 to 8192, as said below
- group_branch: int32 [4], replicated, may hold values from 0 to 3, each once
- guidance_w: float32 [4], replicated, may hold values from -1 to 2
- frame_level: int32 [32], replicated, may hold values from 0 to 31
- residual: bfloat16 [4, 2048, 5120], P('branch', ('seq', 'mp')), may hold values from -0.59765625 to 0.59765625
- out_weight: bfloat16 [2560, 5120], P('mp'), may hold values from -0.75 to 0.75
- mod_table: float32 [32, 2, 5120], replicated, may hold values from -3 to 3
- head_weight: bfloat16 [5120, 64], replicated, may hold values from -0.078125 to 0.078125
Outputs:
- velocity: float32 [2048, 64], P(('seq', 'mp'))
Inputs may be any that keep to these rules, and one draw needn't show every extreme that they name: `hist_len`: one branch attends to all 8192 history tokens and one to none.
All inputs are finite; a program needn't handle non-finite values.
Results may differ from a plain program's by a relative error of at most 0.017.
Values may be sent and summed in bfloat16 or wider, within the bound.
No kernel may reach another device: no remote copies, remote signals or barrier semaphores. Data moves between devices by JAX's collectives and lax.ppermute only.
A program may use at most 128 MiB of HBM per device.

v0:
```python
import jax
import jax.numpy as jnp
from jax import lax
from jax.sharding import PartitionSpec as P

HSZ = 128
FRAME_TOK = 64


NEG = -1e30


def empty_carry(count, heads):
    return (
        jnp.full((count, heads), NEG, jnp.float32),
        jnp.zeros((count, heads), jnp.float32),
        jnp.zeros((count, heads, HSZ), jnp.float32),
    )


def fold_block(carry, queries, keys, values, valid):
    best, total, summed = carry
    heads = queries.shape[1] // HSZ
    q_heads = queries.reshape(queries.shape[0], heads, HSZ)
    k_heads = keys.reshape(keys.shape[0], heads, HSZ)
    v_heads = values.reshape(values.shape[0], heads, HSZ)
    scores = jnp.einsum(
        "qhd,khd->qhk", q_heads, k_heads, preferred_element_type=jnp.float32
    ) * HSZ ** (-0.5)
    scores = jnp.where(valid[None, None, :], scores, NEG)
    peak = jnp.maximum(best, jnp.max(scores, axis=2))
    weights = jnp.where(valid[None, None, :], jnp.exp(scores - peak[:, :, None]), 0.0)
    fade = jnp.exp(best - peak)
    total = total * fade + jnp.sum(weights, axis=2)
    summed = summed * fade[:, :, None] + jnp.einsum(
        "qhk,khd->qhd", weights.astype(jnp.bfloat16), v_heads, preferred_element_type=jnp.float32
    )
    return (peak, total, summed)


def pick(table, index):
    return jnp.sum(jnp.where(jnp.arange(table.shape[0]) == index, table, jnp.zeros_like(table)))


def body(
    span_q,
    span_k,
    span_v,
    hist_k,
    hist_v,
    hist_len,
    group_branch,
    guidance_w,
    frame_level,
    residual,
    out_weight,
    mod_table,
    head_weight,
):
    queries = span_q[0]
    rows = queries.shape[0]
    heads = queries.shape[1] // HSZ
    group = lax.axis_index("branch")
    branch_id = pick(group_branch, group)
    length = pick(hist_len, branch_id)
    weight_now = pick(guidance_w, branch_id)
    pieces = (
        lax.all_gather(span_k[0], "seq", axis=0, tiled=True),
        lax.all_gather(span_v[0], "seq", axis=0, tiled=True),
    )
    valid = jnp.ones((pieces[0].shape[0],), bool)
    carry = fold_block(empty_carry(rows, heads), queries, pieces[0], pieces[1], valid)
    pieces = (
        lax.all_gather(hist_k[0], "seq", axis=0, tiled=True),
        lax.all_gather(hist_v[0], "seq", axis=0, tiled=True),
    )
    valid = jnp.arange(pieces[0].shape[0]) < length
    best, total, summed = fold_block(carry, queries, pieces[0], pieces[1], valid)
    attended = (summed / total[:, :, None]).reshape(rows, heads * HSZ).astype(jnp.bfloat16)
    projected = lax.psum_scatter(
        jnp.dot(attended, out_weight, preferred_element_type=jnp.float32).astype(jnp.bfloat16),
        "mp",
        scatter_dimension=0,
        tiled=True,
    ).astype(jnp.float32)
    stream = residual[0].astype(jnp.float32) + projected
    mean = jnp.mean(stream, axis=1, keepdims=True)
    centred = stream - mean
    variance = jnp.mean(centred * centred, axis=1, keepdims=True)
    normed = centred * lax.rsqrt(variance + 1e-06)
    local_rows = stream.shape[0]
    first_token = lax.axis_index("seq") * rows + lax.axis_index("mp") * local_rows
    frame_index = (first_token + jnp.arange(local_rows)) // FRAME_TOK
    frame_hits = frame_index[:, None] == jnp.arange(frame_level.shape[0])[None, :]
    level_index = jnp.sum(jnp.where(frame_hits, frame_level[None, :], 0), axis=1)
    level_hits = (level_index[:, None] == jnp.arange(mod_table.shape[0])[None, :]).astype(
        jnp.float32
    )
    width = mod_table.shape[2]
    modulation = jnp.dot(
        level_hits,
        mod_table.reshape(mod_table.shape[0], 2 * width),
        precision=lax.Precision.HIGHEST,
        preferred_element_type=jnp.float32,
    )
    shift = modulation[:, :width]
    scale = modulation[:, width:]
    modulated = (normed * (1.0 + scale) + shift).astype(jnp.bfloat16)
    branch_velocity = jnp.dot(modulated, head_weight, preferred_element_type=jnp.float32)
    return lax.psum(weight_now * branch_velocity, "branch")


def solution(mesh):
    in_specs = (
        P("branch", "seq", "mp"),
        P("branch", "seq", "mp"),
        P("branch", "seq", "mp"),
        P("branch", "seq", "mp"),
        P("branch", "seq", "mp"),
        P(),
        P(),
        P(),
        P(),
        P("branch", ("seq", "mp"), None),
        P("mp", None),
        P(),
        P(),
    )
    out_specs = P(("seq", "mp"), None)
    return jax.shard_map(body, mesh=mesh, in_specs=in_specs, out_specs=out_specs, check_vma=False)
```

profile of v0, /device:TPU:24, one launch (start us, length us, event | category | flops | bytes accessed | tf_op | source)
XLA Modules:
  0.0 321.8 jit_solution(12725099809813306328)
XLA Ops:
  6.5 0.0 copy-start
  6.5 0.0 all-gather.11.cloned.1.call-start
  6.5 0.7 all-gather.11.cloned.1.call-update
  7.3 0.0 all-gather.9.cloned.1.call-start
  7.3 1.7 copy.31
  9.0 0.0 all-gather.9.cloned.1.call-update
  9.1 0.0 all-gather.13.cloned.1.call-start
  9.1 2.2 copy.37
  11.3 0.0 all-gather.13.cloned.1.call-update
  11.3 0.0 all-gather.15.cloned.1.call-start
  11.4 0.5 all-gather.15.cloned.1.call-update
  11.9 0.0 reduce-scatter.2.cloned.1.call-start
  11.9 1.1 copy.32
  13.0 1.3 fusion.49
  14.3 1.9 fusion.48
  16.3 0.6 iota_compare_fusion
  16.8 32.6 %all-gather.11.cloned.1.call-done = bf16[1,2048,640]{2,1,0:T(8,128)(2,1)} async-done(((bf16[1,128,640]{2,1,0:T(8,128)(2,1)}), bf16[1,2048,640]{2,1,0:T(8,128)(2,1)}) %all-gather.11.cloned.1.call-update) | async-done | bytes 2621456 | tf_op jit(solution)/shard_map/all_gather | solution.py:69
  49.4 3.0 copy.35
  52.4 40.4 %all-gather.9.cloned.1.call-done = bf16[1,2048,640]{1,2,0:T(8,128)(2,1)} async-done(((bf16[1,128,640]{1,2,0:T(8,128)(2,1)}), bf16[1,2048,640]{1,2,0:T(8,128)(2,1)}) %all-gather.9.cloned.1.call-update) | async-done | bytes 2621456 | tf_op jit(solution)/shard_map/all_gather | solution.py:68
  92.7 5.2 %bitcast_reduce_fusion.1 = (f32[128,5]{0,1:T(8,128)S(1)}, f32[5,2048,128]{2,1,0:T(8,128)}) fusion(bf16[2048,5,128]{0,2,1:T(8,128)(2,1)} %bitcast.82, bf16[128,5,128]{0,2,1:T(8,128)(2,1)S(1)} %bitcast.83), kind=kOutput, calls=%fused_computation.12 | convolution fusion | flops 338165120 | bytes 8030720 | tf_op jit(solution)/shard_map/qhd,khd->qhk/dot_general | solution.py:27
  97.9 61.6 %all-gather.13.cloned.1.call-done = bf16[1,8192,640]{1,2,0:T(8,128)(2,1)} async-done(((bf16[1,512,640]{1,2,0:T(8,128)(2,1)}), bf16[1,8192,640]{1,2,0:T(8,128)(2,1)}) %all-gather.13.cloned.1.call-update) | async-done | bytes 10485776 | tf_op jit(solution)/shard_map/all_gather | solution.py:74
  159.5 0.0 copy-start.1
  159.5 12.8 %bitcast_reduce_fusion = (f32[128,5]{0,1:T(8,128)S(1)}, f32[5,8192,128]{2,1,0:T(8,128)}) fusion(pred[8192]{0:T(1024)(128)(4,1)S(1)} %iota_compare_fusion, bf16[8192,5,128]{0,2,1:T(8,128)(2,1)} %bitcast.78, bf16[128,5,128]{0,2,1:T(8,128)(2,1)S(1)} %bitcast.84), kind=kOutput, calls=%fused_computation.1 | convolution fusion | flops 1357905280 | bytes 31631872 | tf_op jit(solution)/shard_map/qhd,khd->qhk/dot_general | solution.py:27
  172.3 0.0 copy-done.1
  172.3 0.9 fusion.9
  173.1 9.7 %fusion.2 = f32[128,5]{0,1:T(8,128)S(1)} fusion(f32[5,8192,128]{2,1,0:T(8,128)} %get-tuple-element.13, f32[128,5]{0,1:T(8,128)S(1)} %get-tuple-element.8, pred[8192]{0:T(1024)(128)(4,1)S(1)} %iota_compare_fusion), kind=kLoop, calls=%fused_computation.5 | loop fusion | flops 26213760 | bytes 20984832 | tf_op jit(solution)/shard_map/reduce_sum | solution.py:34
  182.8 2.1 fusion.27
  184.9 0.0 copy-start.3
  184.9 41.7 %all-gather.15.cloned.1.call-done = bf16[1,8192,640]{2,1,0:T(8,128)(2,1)} async-done(((bf16[1,512,640]{2,1,0:T(8,128)(2,1)}), bf16[1,8192,640]{2,1,0:T(8,128)(2,1)}) %all-gather.15.cloned.1.call-update) | async-done | bytes 10485776 | tf_op jit(solution)/shard_map/all_gather | solution.py:75
  226.6 0.0 slice-start
  226.6 14.6 %copy.40 = bf16[1,8192,640]{1,2,0:T(8,128)(2,1)} copy(bf16[1,8192,640]{2,1,0:T(8,128)(2,1)} %all-gather.15.cloned.1.call-done) | data formatting | bytes 20971520 | tf_op jit(solution)/shard_map/all_gather | solution.py:75
  241.3 0.0 copy-done.3
  241.3 0.0 slice-start.1
  241.3 13.7 %fusion.33 = bf16[128,5,128]{0,2,1:T(8,128)(2,1)S(1)} fusion(f32[128,5,128]{0,2,1:T(8,128)S(1)} %copy-done.3, bf16[8192,5,128]{0,2,1:T(8,128)(2,1)} %bitcast.79, f32[5,8192,128]{2,1,0:T(8,128)} %get-tuple-element.13, f32[128,5]{0,1:T(8,128)S(1)} %get-tuple-element.8, pred[8192]{0:T(1024)(128)(4,1)S(1)} %iota_compare_fusion, f32[128,5]{0,1:T(8,128)S(1)} %get-tuple-element.5), kind=kOutput, calls=%fused_computation.26 | convolution fusion | flops 1368637440 | bytes 31962112 | tf_op jit(solution)/shard_map/qhk,khd->qhd/dot_general | solution.py:35
  255.0 0.0 slice-done
  255.0 0.0 slice-done.1
  255.0 0.0 copy-start.4
  255.0 0.0 copy-start.5
  255.0 2.3 convolution_convert_fusion
  257.3 0.0 copy-start.2
  257.3 0.0 reduce-scatter.2.cloned.1.call-update
  257.4 1.8 copy.48
  259.2 0.0 copy-done.4
  259.2 1.2 fusion.47
  260.4 0.0 copy-done.5
  260.4 0.2 select_reduce_fusion
  260.6 1.8 fusion.45
  262.4 33.7 %reduce-scatter.2.cloned.1.call-done = bf16[32,5120]{1,0:T(8,128)(2,1)} async-done(((bf16[128,5120]{1,0:T(8,128)(2,1)}), bf16[32,5120]{1,0:T(8,128)(2,1)}) %reduce-scatter.2.cloned.1.call-update) | async-done | bytes 327696 | tf_op jit(solution)/shard_map/reduce_scatter | solution.py:80
  296.1 0.0 copy-done.2
  296.1 1.2 fusion.39
  297.2 1.2 multiply_reduce_fusion
  298.5 0.0 copy-done
  298.5 2.4 convolution_multiply_fusion
  300.8 14.5 %psum.7 = f32[32,64]{1,0:T(8,128)} all-reduce(f32[32,64]{1,0:T(8,128)S(1)} %convolution_multiply_fusion), channel_id=1, replica_groups=mesh['branch'=4,'seq'=16,'mp'=4] {'branch'}, use_global_device_ids=true, to_apply=%region_11.12 | all-reduce | flops 2048 | bytes 16384 | tf_op jit(solution)/shard_map/psum | solution.py:110
  (6 shorter events, 0.0 us)
Async XLA Ops:
  6.5 291.9 %copy-start = (bf16[5120,64]{0,1:T(8,128)(2,1)S(1)}, bf16[5120,64]{0,1:T(8,128)(2,1)}, u32[]{:S(2)}) copy-start(bf16[5120,64]{0,1:T(8,128)(2,1)} %param.25) | copy-start | bytes 1966084
  6.5 42.9 %all-gather.11.cloned.1.call-start = ((), (), s32[]{:S(2)}) async-start(), calls=%async_computation.3 | async-start | bytes 2785280 | tf_op jit(solution)/shard_map/all_gather | solution.py:69
  7.3 85.5 %all-gather.9.cloned.1.call-start = ((), (), s32[]{:S(2)}) async-start(), calls=%async_computation.2 | async-start | bytes 2785280 | tf_op jit(solution)/shard_map/all_gather | solution.py:68
  9.1 150.4 %all-gather.13.cloned.1.call-start = ((), (), s32[]{:S(2)}) async-start(), calls=%async_computation.4 | async-start | bytes 11141120 | tf_op jit(solution)/shard_map/all_gather | solution.py:74
  11.3 215.3 %all-gather.15.cloned.1.call-start = ((), (), s32[]{:S(2)}) async-start(), calls=%async_computation.5 | async-start | bytes 11141120 | tf_op jit(solution)/shard_map/all_gather | solution.py:75
  11.9 284.2 %reduce-scatter.2.cloned.1.call-start = ((), (), s32[]{:S(2)}) async-start(), calls=%async_computation.1 | async-start | bytes 1638400 | tf_op jit(solution)/shard_map/reduce_scatter | solution.py:80
  159.5 12.8 %copy-start.1 = (f32[5,2048,128]{2,1,0:T(8,128)S(1)}, f32[5,2048,128]{2,1,0:T(8,128)}, u32[]{:S(2)}) copy-start(f32[5,2048,128]{2,1,0:T(8,128)} %get-tuple-element.11) | copy-start | bytes 15728644
  184.9 56.3 %copy-start.3 = (f32[128,5,128]{0,2,1:T(8,128)S(1)}, f32[128,5,128]{0,2,1:T(8,128)}, u32[]{:S(2)}) copy-start(f32[128,5,128]{0,2,1:T(8,128)} %fusion.27) | copy-start | bytes 983044
  226.6 28.4 %slice-start = ((s8[6553600]{0:T(1024)(128)(4,1)}), s8[2359296]{0:T(1024)(128)(4,1)S(1)}, s32[]{:S(2)}) async-start(s8[6553600]{0:T(1024)(128)(4,1)} %bitcast.76), calls=%async_computation.6 | async-start | bytes 4718592
  241.3 13.7 %slice-start.1 = ((s8[6553600]{0:T(1024)(128)(4,1)}), s8[4194304]{0:T(1024)(128)(4,1)S(1)}, s32[]{:S(2)}) async-start(s8[6553600]{0:T(1024)(128)(4,1)} %bitcast.76), calls=%async_computation.7 | async-start | bytes 8388608
  255.0 4.2 %copy-start.4 = (f32[4]{0:T(128)S(1)}, f32[4]{0:T(128)}, u32[]{:S(2)}) copy-start(f32[4]{0:T(128)} %param.20) | copy-start | bytes 52
  255.0 5.4 %copy-start.5 = (s32[32]{0:T(128)S(1)}, s32[32]{0:T(128)}, u32[]{:S(2)}) copy-start(s32[32]{0:T(128)} %param.21) | copy-start | bytes 388
  257.3 38.7 %copy-start.2 = (bf16[1,32,5120]{2,1,0:T(8,128)(2,1)S(1)}, bf16[1,32,5120]{2,1,0:T(8,128)(2,1)}, u32[]{:S(2)}) copy-start(bf16[1,32,5120]{2,1,0:T(8,128)(2,1)} %param.22) | copy-start | bytes 983044
Sparse Core Ops, SparseCore 0:
  9.2 40.1 all-gather.10
  51.2 41.5 all-gather.8
  94.6 64.8 all-gather.12
  161.2 65.4 all-gather.14
  257.5 38.5 reduce-scatter.1
where the time goes:
time: 326 us; the launch traced here: 322 us
  waiting for transfers between devices  211 us (65%)
  matrix products  40.2 us (12%)
  local copies, waits for them, and re-layouts  24.4 us (7%)
  other arithmetic  18.2 us (6%)
  blocking collectives  14.5 us (4%)
  between operations  13.3 us (4%)
    all_gather x1, waiting for transfers between devices, body(): lax.all_gather(hist_k[0], 'seq', axis=0, tiled=True)  61.6 us
    all_gather x1, waiting for transfers between devices, body(): lax.all_gather(hist_v[0], 'seq', axis=0, tiled=True)  41.7 us
    all_gather x1, waiting for transfers between devices, body(): lax.all_gather(span_k[0], 'seq', axis=0, tiled=True)  40.4 us
    reduce_scatter x1, waiting for transfers between devices, body(): lax.psum_scatter(jnp.dot(attended, out_weight, preferred_element_type=jnp...  33.7 us
    all_gather x1, waiting for transfers between devices, body(): lax.all_gather(span_v[0], 'seq', axis=0, tiled=True)  32.6 us
    dot_general x2, matrix products, fold_block(): jnp.einsum('qhd,khd->qhk', q_heads, k_heads, preferred_element_type=jnp.f...  18 us
    dot_general x2, matrix products, fold_block(): jnp.einsum('qhk,khd->qhd', weights.astype(jnp.bfloat16), v_heads, preferr...  15.8 us
    all_gather x1, local copies, waits for them, and re-layouts, body(): lax.all_gather(hist_v[0], 'seq', axis=0, tiled=True)  14.6 us
  transfers between devices with their start and end apart: 5, of which 5 were waited for; matrix products, arithmetic and copies ran while one was open for 15% of the time, Pallas kernels for 0%

commit v1 on v0

v1 whole, which is shorter than its diff:
```python
import functools

import jax
import jax.numpy as jnp
from jax import lax
from jax.experimental import pallas as pl
from jax.experimental.pallas import tpu as pltpu
from jax.sharding import PartitionSpec as P

HSZ = 128
FRAME_TOK = 64
NEG = -1e30
STAT_ROWS = 16
SCORE_TO_EXP2 = HSZ ** (-0.5) * 1.4426950408889634

XS = 4


def hop(dz, dx, dc):
    return [
        ((z * XS + x) * 2 + c, ((z ^ dz) * XS + (x + dx) % XS) * 2 + (c ^ dc))
        for z in range(2)
        for x in range(XS)
        for c in range(2)
    ]


def turn(step, count=4):
    return [(i, (i + step) % count) for i in range(count)]


def attend_kernel(blocks, width, hist_len, group_branch, *refs):
    queries = refs[:blocks]
    keys = refs[blocks : blocks + 4]
    values = refs[blocks + 4 : blocks + 8]
    sent = refs[blocks + 8 : 2 * blocks + 8]
    turned = refs[2 * blocks + 8]
    rows, feat = queries[0].shape
    heads = feat // HSZ
    sizes = [k.shape[0] for k in keys]
    length = hist_len[group_branch[lax.axis_index("branch")]]
    seq = lax.axis_index("seq")
    other = seq + 1 - 2 * lax.rem(seq, 2)
    for h in range(heads):
        cols = slice(h * HSZ, (h + 1) * HSZ)
        at = 0
        for value, size in zip(values, sizes):
            turned[cols, at : at + size] = value[:, cols].T
            at += size
    for first in range(0, blocks, width):
        stats = []
        for h in range(heads):
            cols = slice(h * HSZ, (h + 1) * HSZ)
            q = jnp.concatenate([queries[first + i][:, cols] for i in range(width)], axis=0)
            scores = []
            for j, key in enumerate(keys):
                s = lax.dot_general(
                    key[:, cols], q, (((1,), (1,)), ((), ())), preferred_element_type=jnp.float32
                )
                if j >= 2:
                    start = (seq if j == 2 else other) * sizes[j]
                    spot = start + lax.broadcasted_iota(jnp.int32, s.shape, 0)
                    s = jnp.where(spot < length, s, NEG)
                scores.append(s)
            peak = functools.reduce(
                jnp.maximum, [jnp.max(s, axis=0, keepdims=True) for s in scores]
            )
            total, summed, at = 0.0, 0.0, 0
            for s, size in zip(scores, sizes):
                weight = jnp.exp2((s - peak) * SCORE_TO_EXP2)
                total = total + jnp.sum(weight, axis=0, keepdims=True)
                summed = summed + jnp.dot(
                    turned[cols, at : at + size],
                    weight.astype(jnp.bfloat16),
                    preferred_element_type=jnp.float32,
                )
                at += size
            out = (summed / total).astype(jnp.bfloat16)
            for i in range(width):
                sent[first + i][cols, :] = out[:, i * rows : (i + 1) * rows]
            level = peak * SCORE_TO_EXP2 + jnp.log2(total)
            high = level.astype(jnp.bfloat16).astype(jnp.float32)
            middle = (level - high).astype(jnp.bfloat16).astype(jnp.float32)
            stats += [high, middle, level - high - middle]
        stats.append(jnp.zeros((STAT_ROWS - len(stats), stats[0].shape[1]), jnp.float32))
        stats = jnp.concatenate(stats, axis=0).astype(jnp.bfloat16)
        for i in range(width):
            sent[first + i][feat:, :] = stats[:, i * rows : (i + 1) * rows]


def attend(hist_len, group_branch, queries, keys, values, width):
    blocks = len(queries)
    rows, feat = queries[0].shape
    count = sum(k.shape[0] for k in keys)
    vmem = pl.BlockSpec(memory_space=pltpu.VMEM)
    smem = pl.BlockSpec(memory_space=pltpu.SMEM)
    return pl.pallas_call(
        functools.partial(attend_kernel, blocks, width),
        out_shape=[jax.ShapeDtypeStruct((feat + STAT_ROWS, rows), jnp.bfloat16)] * blocks,
        in_specs=[smem, smem] + [vmem] * (blocks + 8),
        out_specs=[vmem] * blocks,
        scratch_shapes=[pltpu.VMEM((feat, count), jnp.bfloat16)],
        compiler_params=pltpu.CompilerParams(vmem_limit_bytes=40 * 2**20),
        cost_estimate=pl.CostEstimate(
            flops=4 * blocks * rows * count * feat,
            bytes_accessed=4 * count * feat,
            transcendentals=blocks * rows * count * (feat // HSZ),
        ),
        name="attend",
    )(hist_len, group_branch, *queries, *keys, *values)


def project_kernel(count, *refs):
    parts = refs[:count]
    weight = refs[count]
    outs = refs[count + 1 : count + 5]
    held = refs[count + 5]
    feat = weight.shape[0]
    heads = feat // HSZ
    stats = [part[feat:, :].astype(jnp.float32) for part in parts]
    for h in range(heads):
        rows = slice(h * HSZ, (h + 1) * HSZ)
        levels = [
            s[3 * h : 3 * h + 1] + s[3 * h + 1 : 3 * h + 2] + s[3 * h + 2 : 3 * h + 3] for s in stats
        ]
        peak = functools.reduce(jnp.maximum, levels)
        shares = [jnp.exp2(level - peak) for level in levels]
        total = functools.reduce(jnp.add, shares)
        summed = functools.reduce(
            jnp.add, [part[rows, :].astype(jnp.float32) * share for part, share in zip(parts, shares)]
        )
        held[:, rows] = (summed / total).T
    mine = lax.axis_index("mp")
    step = outs[0].shape[0]
    for k, out in enumerate(outs):
        start = pl.multiple_of(lax.rem(mine + k, 4) * step, step)
        attended = held[pl.ds(start, step), :].astype(jnp.bfloat16)
        out[...] = jnp.dot(attended, weight[...], preferred_element_type=jnp.float32).astype(
            out.dtype
        )


def project(parts, weight):
    feat, width = weight.shape
    rows = parts[0].shape[1]
    vmem = pl.BlockSpec(memory_space=pltpu.VMEM)
    return pl.pallas_call(
        functools.partial(project_kernel, len(parts)),
        out_shape=[jax.ShapeDtypeStruct((rows // 4, width), jnp.bfloat16)] * 4,
        in_specs=[vmem] * (len(parts) + 1),
        out_specs=[vmem] * 4,
        scratch_shapes=[pltpu.VMEM((rows, feat), jnp.float32)],
        compiler_params=pltpu.CompilerParams(vmem_limit_bytes=40 * 2**20),
        cost_estimate=pl.CostEstimate(
            flops=2 * rows * feat * width, bytes_accessed=2 * feat * width, transcendentals=0
        ),
        name="project",
    )(*parts, weight)


def head_kernel(
    group_branch, guidance_w, frame_level, p0, p1, p2, p3, residual, table, weight, out, held, sem
):
    rows, width = residual.shape
    token = (lax.axis_index("seq") * 4 + lax.axis_index("mp")) * rows
    level = frame_level[token // FRAME_TOK]
    fetch = pltpu.make_async_copy(table.at[level], held, sem)
    fetch.start()
    stream = residual[...].astype(jnp.float32) + (
        (p0[...].astype(jnp.float32) + p1[...].astype(jnp.float32))
        + (p2[...].astype(jnp.float32) + p3[...].astype(jnp.float32))
    )
    mean = jnp.mean(stream, axis=1, keepdims=True)
    centred = stream - mean
    variance = jnp.mean(centred * centred, axis=1, keepdims=True)
    normed = centred * lax.rsqrt(variance + 1e-06)
    fetch.wait()
    modulated = (normed * (1.0 + held[1:2, :]) + held[0:1, :]).astype(jnp.bfloat16)
    velocity = jnp.dot(modulated, weight[...], preferred_element_type=jnp.float32)
    out[...] = velocity * guidance_w[group_branch[lax.axis_index("branch")]]


def head(group_branch, guidance_w, frame_level, parts, residual, table, weight):
    rows, width = residual.shape
    vmem = pl.BlockSpec(memory_space=pltpu.VMEM)
    smem = pl.BlockSpec(memory_space=pltpu.SMEM)
    return pl.pallas_call(
        head_kernel,
        out_shape=jax.ShapeDtypeStruct((rows, weight.shape[1]), jnp.float32),
        in_specs=[smem] * 3 + [vmem] * 5 + [pl.BlockSpec(memory_space=pl.ANY), vmem],
        out_specs=vmem,
        scratch_shapes=[pltpu.VMEM(table.shape[1:], jnp.float32), pltpu.SemaphoreType.DMA],
        compiler_params=pltpu.CompilerParams(vmem_limit_bytes=40 * 2**20),
        name="head",
    )(group_branch, guidance_w, frame_level, *parts, residual, table, weight)


def body(
    span_q,
    span_k,
    span_v,
    hist_k,
    hist_v,
    hist_len,
    group_branch,
    guidance_w,
    frame_level,
    residual,
    out_weight,
    mod_table,
    head_weight,
):
    q = span_q[0]
    moves = [(0, 0), (1, 0), (0, 1), (0, 3), (1, 1), (1, 3), (0, 2), (1, 2)]
    queries = [q if m == (0, 0) else lax.ppermute(q, "seq", hop(*m, 0)) for m in moves]
    mine = [span_k[0], span_v[0], hist_k[0], hist_v[0]]
    theirs = [lax.ppermute(a, "seq", hop(0, 0, 1)) for a in mine]
    keys = [mine[0], theirs[0], mine[2], theirs[2]]
    values = [mine[1], theirs[1], mine[3], theirs[3]]
    partial = attend(hist_len, group_branch, queries[:4], keys, values, 4)
    partial += attend(hist_len, group_branch, queries[4:], keys, values, 4)
    parts = [
        p if m == (0, 0) else lax.ppermute(p, "seq", hop(m[0], -m[1], 0))
        for m, p in zip(moves, partial)
    ]
    blocks = project(parts, out_weight)
    reduced = [blocks[0]] + [lax.ppermute(blocks[k], "mp", turn(k)) for k in (1, 3, 2)]
    velocity = head(
        group_branch, guidance_w, frame_level, reduced, residual[0], mod_table, head_weight
    )
    around = [lax.ppermute(velocity, "branch", turn(k)) for k in (1, 3, 2)]
    return (velocity + around[2]) + (around[0] + around[1])


def solution(mesh):
    in_specs = (
        P("branch", "seq", "mp"),
        P("branch", "seq", "mp"),
        P("branch", "seq", "mp"),
        P("branch", "seq", "mp"),
        P("branch", "seq", "mp"),
        P(),
        P(),
        P(),
        P(),
        P("branch", ("seq", "mp"), None),
        P("mp", None),
        P(),
        P(),
    )
    out_specs = P(("seq", "mp"), None)
    return jax.shard_map(body, mesh=mesh, in_specs=in_specs, out_specs=out_specs, check_vma=False)
```

time: 326 us -> 116 us (0.36)
  the two profiles are of different devices: /device:TPU:24 before, /device:TPU:56 now
where the time goes in v1:
time: 116 us
  waiting for transfers between devices  44.4 us (38%)
  starting transfers between devices  37.5 us (32%)
  Pallas kernels  21 us (18%)
  local copies, waits for them, and re-layouts  11.9 us (10%)
    ppermute x3, waiting for transfers between devices, body(): lax.ppermute(blocks[k], 'mp', turn(k))  23.3 us
    pallas_call x2, Pallas kernels, attend(): pl.pallas_call(functools.partial(attend_kernel, blocks, width), out_shape...  13.2 us
    unnamed x35, local copies, waits for them, and re-layouts  11.9 us
    ppermute x7, starting transfers between devices, body(): lax.ppermute(q, 'seq', hop(*m, 0))  11.7 us
    ppermute x3, starting transfers between devices, body(): lax.ppermute(blocks[k], 'mp', turn(k))  11.7 us
    ppermute x7, starting transfers between devices, body(): lax.ppermute(p, 'seq', hop(m[0], -m[1], 0))  10.1 us
    ppermute x7, waiting for transfers between devices, body(): lax.ppermute(q, 'seq', hop(*m, 0))  9.83 us
    ppermute x7, waiting for transfers between devices, body(): lax.ppermute(p, 'seq', hop(m[0], -m[1], 0))  6.32 us
  transfers between devices with their start and end apart: 24, of which 11 were waited for; matrix products, arithmetic and copies ran while one was open for 1% of the time, Pallas kernels for 11%

profile of v1, /device:TPU:56, one launch (start us, length us, event | category | flops | bytes accessed | tf_op | source)
XLA Modules:
  0.0 115.5 jit_solution(16238821805566650065)
XLA Ops:
  0.0 0.0 collective-permute-start.4
  0.0 0.5 collective-permute-start.6
  0.5 1.0 collective-permute-start.10
  1.5 3.1 %collective-permute-start.11 = (bf16[128,640]{1,0:T(8,128)(2,1)}, bf16[128,640]{1,0:T(8,128)(2,1)S(1)}, u32[]{:S(2)}, u32[]{:S(2)}) collective-permute-start(bf16[128,640]{1,0:T(8,128)(2,1)} %bitcast.14), channel_id=1, source_target_pairs={{0,56},{4,60},{8,32},{12,36},{16,40},{20,44},{24,48},{28,52},{32,2... | collective-permute-start | bytes 491528 | tf_op jit(solution)/shard_map/ppermute | solution.py:215
  4.6 1.8 %collective-permute-start.12 = (bf16[128,640]{1,0:T(8,128)(2,1)}, bf16[128,640]{1,0:T(8,128)(2,1)S(1)}, u32[]{:S(2)}, u32[]{:S(2)}) collective-permute-start(bf16[128,640]{1,0:T(8,128)(2,1)} %bitcast.15), channel_id=1, source_target_pairs={{0,16},{4,20},{8,24},{12,28},{16,0},{20,4},{24,8},{28,12},{32,48},... | collective-permute-start | bytes 491528 | tf_op jit(solution)/shard_map/ppermute | solution.py:215
  6.5 3.4 %collective-permute-done.10.refs_0_ = bf16[128,640]{1,0:T(8,128)(2,1)S(1)} collective-permute-done((bf16[128,640]{1,0:T(8,128)(2,1)}, bf16[128,640]{1,0:T(8,128)(2,1)S(1)}, u32[]{:S(2)}, u32[]{:S(2)}) %collective-permute-start.10) | collective-permute-done | bytes 163872 | tf_op jit(solution)/shard_map/ppermute | solution.py:215
  9.9 1.5 %collective-permute-start.13 = (bf16[128,640]{1,0:T(8,128)(2,1)}, bf16[128,640]{1,0:T(8,128)(2,1)S(1)}, u32[]{:S(2)}, u32[]{:S(2)}) collective-permute-start(bf16[128,640]{1,0:T(8,128)(2,1)} %bitcast.16), channel_id=1, source_target_pairs={{0,48},{4,52},{8,56},{12,60},{16,32},{20,36},{24,40},{28,44},{32,1... | collective-permute-start | bytes 491528 | tf_op jit(solution)/shard_map/ppermute | solution.py:215
  11.4 0.9 collective-permute-done.11.refs_1_
  12.3 0.0 collective-permute-start.3
  12.3 1.2 %collective-permute-done.12.refs_2_ = bf16[128,640]{1,0:T(8,128)(2,1)S(1)} collective-permute-done((bf16[128,640]{1,0:T(8,128)(2,1)}, bf16[128,640]{1,0:T(8,128)(2,1)S(1)}, u32[]{:S(2)}, u32[]{:S(2)}) %collective-permute-start.12) | collective-permute-done | bytes 163872 | tf_op jit(solution)/shard_map/ppermute | solution.py:215
  13.5 0.0 collective-permute-start.5
  13.5 4.3 %collective-permute-done.13.refs_3_ = bf16[128,640]{1,0:T(8,128)(2,1)S(1)} collective-permute-done((bf16[128,640]{1,0:T(8,128)(2,1)}, bf16[128,640]{1,0:T(8,128)(2,1)S(1)}, u32[]{:S(2)}, u32[]{:S(2)}) %collective-permute-start.13) | collective-permute-done | bytes 163872 | tf_op jit(solution)/shard_map/ppermute | solution.py:215
  17.8 0.1 collective-permute-start
  17.9 0.0 collective-permute-done.3.refs_5_
  17.9 1.6 %collective-permute-start.1 = (bf16[128,640]{1,0:T(8,128)(2,1)}, bf16[128,640]{1,0:T(8,128)(2,1)S(1)}, u32[]{:S(2)}, u32[]{:S(2)}) collective-permute-start(bf16[128,640]{1,0:T(8,128)(2,1)} %bitcast.18), channel_id=1, source_target_pairs={{0,8},{4,12},{8,16},{12,20},{16,24},{20,28},{24,0},{28,4},{32,40},... | collective-permute-start | bytes 491528 | tf_op jit(solution)/shard_map/ppermute | solution.py:215
  19.5 0.0 collective-permute-done.5.refs_9_
  19.5 2.5 %collective-permute-start.2 = (bf16[128,640]{1,0:T(8,128)(2,1)}, bf16[128,640]{1,0:T(8,128)(2,1)S(1)}, u32[]{:S(2)}, u32[]{:S(2)}) collective-permute-start(bf16[128,640]{1,0:T(8,128)(2,1)} %bitcast.19), channel_id=1, source_target_pairs={{0,24},{4,28},{8,0},{12,4},{16,8},{20,12},{24,16},{28,20},{32,56},... | collective-permute-start | bytes 491528 | tf_op jit(solution)/shard_map/ppermute | solution.py:215
  22.1 0.0 collective-permute-done.4.refs_7_
  22.1 0.0 collective-permute-done.6.refs_11_
  22.1 0.7 copy-done.3
  22.8 1.1 copy-done.7
  23.8 1.1 copy-done.9
  24.9 0.9 copy-done.12
  25.8 0.9 copy-done.14
  26.8 0.7 copy-done.16
  27.4 6.6 %attend.3 = (bf16[656,128]{1,0:T(8,128)(2,1)S(1)}, bf16[656,128]{1,0:T(8,128)(2,1)S(1)}, bf16[656,128]{1,0:T(8,128)(2,1)S(1)}, bf16[656,128]{1,0:T(8,128)(2,1)S(1)}) custom-call(s32[4]{0:T(128)S(1)} %copy-done.16, s32[4]{0:T(128)S(1)} %copy-done.3, bf16[128,640]{1,0:T(8,128)(2,1)S(1)} %collective-permute-done.10.refs_0_, ...), custom_call_target="tpu_custom_call" | custom-call | flops 1677721600 | bytes 3276800 | tf_op jit(solution)/shard_map/attend/pallas_call | solution.py:97
  34.0 2.0 %collective-permute-start.14 = (bf16[656,128]{1,0:T(8,128)(2,1)S(1)}, bf16[656,128]{1,0:T(8,128)(2,1)S(1)}, u32[]{:S(2)}, u32[]{:S(2)}) collective-permute-start(bf16[656,128]{1,0:T(8,128)(2,1)S(1)} %get-tuple-element.21), channel_id=1, source_target_pairs={{0,56},{4,60},{8,32},{12,36},{16,40},{20,44},{24,48},{28,52},{32,2... | collective-permute-start | bytes 503816 | tf_op jit(solution)/shard_map/ppermute | solution.py:223
  36.0 1.0 collective-permute-start.15
  37.0 0.0 collective-permute-done.refs_1_
  37.0 0.9 collective-permute-start.16
  37.9 0.0 collective-permute-done.1.refs_2_
  37.9 3.1 %collective-permute-start.17 = (bf16[656,128]{1,0:T(8,128)(2,1)S(1)}, bf16[656,128]{1,0:T(8,128)(2,1)S(1)}, u32[]{:S(2)}, u32[]{:S(2)}) collective-permute-start(bf16[656,128]{1,0:T(8,128)(2,1)S(1)} %get-tuple-element.24), channel_id=1, source_target_pairs={{0,48},{4,52},{8,56},{12,60},{16,32},{20,36},{24,40},{28,44},{32,1... | collective-permute-start | bytes 503816 | tf_op jit(solution)/shard_map/ppermute | solution.py:223
  41.0 0.0 collective-permute-done.2.refs_3_
  41.0 1.1 copy-done.8
  42.1 1.1 copy-done.10
  43.2 0.9 copy-done.11
  44.1 0.9 copy-done.13
  45.1 0.9 copy-done.15
  46.0 6.6 %attend.2 = (bf16[656,128]{1,0:T(8,128)(2,1)S(1)}, bf16[656,128]{1,0:T(8,128)(2,1)S(1)}, bf16[656,128]{1,0:T(8,128)(2,1)S(1)}, bf16[656,128]{1,0:T(8,128)(2,1)S(1)}) custom-call(s32[4]{0:T(128)S(1)} %copy-done.16, s32[4]{0:T(128)S(1)} %copy-done.3, bf16[128,640]{1,0:T(8,128)(2,1)S(1)} %bitcast.20, bf16[128,640]{1,0:T(8,128)(2,1)S(1)} %collective-permute-done.refs_1_, ...), custom_call_target="tpu_custom_call" | custom-call | flops 1677721600 | bytes 3276800 | tf_op jit(solution)/shard_map/attend/pallas_call | solution.py:97
  52.6 1.1 collective-permute-start.7
  53.6 0.0 collective-permute-done.14.refs_4_
  53.7 1.8 %collective-permute-start.8 = (bf16[656,128]{1,0:T(8,128)(2,1)S(1)}, bf16[656,128]{1,0:T(8,128)(2,1)S(1)}, u32[]{:S(2)}, u32[]{:S(2)}) collective-permute-start(bf16[656,128]{1,0:T(8,128)(2,1)S(1)} %get-tuple-element.19), channel_id=1, source_target_pairs={{0,24},{4,28},{8,0},{12,4},{16,8},{20,12},{24,16},{28,20},{32,56},... | collective-permute-start | bytes 503816 | tf_op jit(solution)/shard_map/ppermute | solution.py:223
  55.4 0.0 collective-permute-done.15.refs_5_
  55.4 0.3 collective-permute-start.9
  55.7 2.3 %collective-permute-done.7.refs_1_ = bf16[656,128]{1,0:T(8,128)(2,1)S(1)} collective-permute-done((bf16[656,128]{1,0:T(8,128)(2,1)S(1)}, bf16[656,128]{1,0:T(8,128)(2,1)S(1)}, u32[]{:S(2)}, u32[]{:S(2)}) %collective-permute-start.7) | collective-permute-done | bytes 167968 | tf_op jit(solution)/shard_map/ppermute | solution.py:223
  58.0 1.0 collective-permute-done.8.refs_2_
  59.0 3.0 %collective-permute-done.9.refs_3_ = bf16[656,128]{1,0:T(8,128)(2,1)S(1)} collective-permute-done((bf16[656,128]{1,0:T(8,128)(2,1)S(1)}, bf16[656,128]{1,0:T(8,128)(2,1)S(1)}, u32[]{:S(2)}, u32[]{:S(2)}) %collective-permute-start.9) | collective-permute-done | bytes 167968 | tf_op jit(solution)/shard_map/ppermute | solution.py:223
  62.0 5.7 %project.1 = (bf16[32,5120]{1,0:T(8,128)(2,1)S(1)}, bf16[32,5120]{1,0:T(8,128)(2,1)}, bf16[32,5120]{1,0:T(8,128)(2,1)}, bf16[32,5120]{1,0:T(8,128)(2,1)}) custom-call(bf16[656,128]{1,0:T(8,128)(2,1)S(1)} %get-tuple-element.17.refs_0_, bf16[656,128]{1,0:T(8,128)(2,1)S(1)} %collective-permute-done.7.refs_1_, ...), custom_call_target="tpu_custom_call" | custom-call | flops 838860800 | bytes 6553600 | tf_op jit(solution)/shard_map/project/pallas_call | solution.py:147
  67.7 0.0 copy-start.6
  67.7 3.6 %collective-permute-start.18 = (bf16[32,5120]{1,0:T(8,128)(2,1)}, bf16[32,5120]{1,0:T(8,128)(2,1)}, u32[]{:S(2)}, u32[]{:S(2)}) collective-permute-start(bf16[32,5120]{1,0:T(8,128)(2,1)} %get-tuple-element.26), channel_id=1, source_target_pairs={{0,1},{1,2},{2,3},{3,0},{4,5},{5,6},{6,7},{7,4},{8,9},{9,10},{10,1... | collective-permute-start | bytes 983048 | tf_op jit(solution)/shard_map/ppermute | solution.py:227
  71.3 3.1 %collective-permute-start.19 = (bf16[32,5120]{1,0:T(8,128)(2,1)}, bf16[32,5120]{1,0:T(8,128)(2,1)}, u32[]{:S(2)}, u32[]{:S(2)}) collective-permute-start(bf16[32,5120]{1,0:T(8,128)(2,1)} %get-tuple-element.27), channel_id=1, source_target_pairs={{0,3},{1,0},{2,1},{3,2},{4,7},{5,4},{6,5},{7,6},{8,11},{9,8},{10,9... | collective-permute-start | bytes 983048 | tf_op jit(solution)/shard_map/ppermute | solution.py:227
  74.4 5.0 %collective-permute-start.20 = (bf16[32,5120]{1,0:T(8,128)(2,1)}, bf16[32,5120]{1,0:T(8,128)(2,1)}, u32[]{:S(2)}, u32[]{:S(2)}) collective-permute-start(bf16[32,5120]{1,0:T(8,128)(2,1)} %get-tuple-element.28), channel_id=1, source_target_pairs={{0,2},{1,3},{2,0},{3,1},{4,6},{5,7},{6,4},{7,5},{8,10},{9,11},{10,... | collective-permute-start | bytes 983048 | tf_op jit(solution)/shard_map/ppermute | solution.py:227
  79.4 1.7 %copy.14.weight = bf16[5120,64]{1,0:T(8,128)(2,1)S(1)} copy(bf16[5120,64]{0,1:T(8,128)(2,1)} %param.25) | data formatting | bytes 1310720 | tf_op args[12]
  81.1 13.4 %collective-permute-done.18.p1 = bf16[32,5120]{1,0:T(8,128)(2,1)} collective-permute-done((bf16[32,5120]{1,0:T(8,128)(2,1)}, bf16[32,5120]{1,0:T(8,128)(2,1)}, u32[]{:S(2)}, u32[]{:S(2)}) %collective-permute-start.18) | collective-permute-done | bytes 327712 | tf_op jit(solution)/shard_map/ppermute | solution.py:227
  94.5 0.0 collective-permute-done.19.p2
  94.5 9.9 %collective-permute-done.20.p3 = bf16[32,5120]{1,0:T(8,128)(2,1)} collective-permute-done((bf16[32,5120]{1,0:T(8,128)(2,1)}, bf16[32,5120]{1,0:T(8,128)(2,1)}, u32[]{:S(2)}, u32[]{:S(2)}) %collective-permute-start.20) | collective-permute-done | bytes 327712 | tf_op jit(solution)/shard_map/ppermute | solution.py:227
  104.4 2.0 %head.1 = f32[32,64]{1,0:T(8,128)S(1)} custom-call(s32[4]{0:T(128)S(1)} %copy-done.4, f32[4]{0:T(128)S(1)} %copy-done.5, s32[32]{0:T(128)S(1)} %copy-done.6, bf16[32,5120]{1,0:T(8,128)(2,1)S(1)} %get-tuple-element.25.p0, bf16[32,5120]{1,0:T(8,128)(2,1)} %collective-permute-done.18.p1, bf16[32,5120]{1,0:T(8,128)(2,1)} %collective-permute-done.19.p2, ...), custom_call_target="tpu_custom_call" | custom-call | tf_op jit(solution)/shard_map/head/pallas_call | solution.py:187
  106.5 1.3 %collective-permute-start.21 = (f32[32,64]{1,0:T(8,128)S(1)}, f32[32,64]{1,0:T(8,128)S(1)}, u32[]{:S(2)}, u32[]{:S(2)}) collective-permute-start(f32[32,64]{1,0:T(8,128)S(1)} %head.1), channel_id=1, source_target_pairs={{0,128},{64,192},{128,0},{192,64},{1,129},{65,193},{129,1},{193,65... | collective-permute-start | bytes 24584 | tf_op jit(solution)/shard_map/ppermute | solution.py:231
  107.8 2.2 %collective-permute-start.22 = (f32[32,64]{1,0:T(8,128)S(1)}, f32[32,64]{1,0:T(8,128)S(1)}, u32[]{:S(2)}, u32[]{:S(2)}) collective-permute-start(f32[32,64]{1,0:T(8,128)S(1)} %head.1), channel_id=1, source_target_pairs={{0,64},{64,128},{128,192},{192,0},{1,65},{65,129},{129,193},{193,1... | collective-permute-start | bytes 24584 | tf_op jit(solution)/shard_map/ppermute | solution.py:231
  110.0 0.0 collective-permute-start.23
  110.0 1.8 %collective-permute-done.21 = f32[32,64]{1,0:T(8,128)S(1)} collective-permute-done((f32[32,64]{1,0:T(8,128)S(1)}, f32[32,64]{1,0:T(8,128)S(1)}, u32[]{:S(2)}, u32[]{:S(2)}) %collective-permute-start.21) | collective-permute-done | bytes 8224 | tf_op jit(solution)/shard_map/ppermute | solution.py:231
  111.8 0.0 collective-permute-done.22
  111.8 3.1 %collective-permute-done.23 = f32[32,64]{1,0:T(8,128)S(1)} collective-permute-done((f32[32,64]{1,0:T(8,128)S(1)}, f32[32,64]{1,0:T(8,128)S(1)}, u32[]{:S(2)}, u32[]{:S(2)}) %collective-permute-start.23) | collective-permute-done | bytes 8224 | tf_op jit(solution)/shard_map/ppermute | solution.py:231
  114.9 0.6 add_add_fusion
  (24 shorter events, 0.0 us)
Async XLA Ops:
  0.0 22.1 %collective-permute-start.4 = (bf16[512,640]{1,0:T(8,128)(2,1)}, bf16[512,640]{1,0:T(8,128)(2,1)S(1)}, u32[]{:S(2)}, u32[]{:S(2)}) collective-permute-start(bf16[512,640]{1,0:T(8,128)(2,1)} %bitcast.7), channel_id=1, source_target_pairs={{0,4},{4,0},{8,12},{12,8},{16,20},{20,16},{24,28},{28,24},{32,36},... | collective-permute-start | bytes 1966088 | tf_op jit(solution)/shard_map/ppermute | solution.py:217
  0.0 22.1 %collective-permute-start.6 = (bf16[512,640]{1,0:T(8,128)(2,1)}, bf16[512,640]{1,0:T(8,128)(2,1)S(1)}, u32[]{:S(2)}, u32[]{:S(2)}) collective-permute-start(bf16[512,640]{1,0:T(8,128)(2,1)} %bitcast.10), channel_id=1, source_target_pairs={{0,4},{4,0},{8,12},{12,8},{16,20},{20,16},{24,28},{28,24},{32,36},... | collective-permute-start | bytes 1966088 | tf_op jit(solution)/shard_map/ppermute | solution.py:217
  0.5 9.4 %collective-permute-start.10 = (bf16[128,640]{1,0:T(8,128)(2,1)}, bf16[128,640]{1,0:T(8,128)(2,1)S(1)}, u32[]{:S(2)}, u32[]{:S(2)}) collective-permute-start(bf16[128,640]{1,0:T(8,128)(2,1)} %bitcast.13), channel_id=1, source_target_pairs={{0,40},{4,44},{8,48},{12,52},{16,56},{20,60},{24,32},{28,36},{32,8... | collective-permute-start | bytes 491528 | tf_op jit(solution)/shard_map/ppermute | solution.py:215
  1.5 10.8 %collective-permute-start.11 = (bf16[128,640]{1,0:T(8,128)(2,1)}, bf16[128,640]{1,0:T(8,128)(2,1)S(1)}, u32[]{:S(2)}, u32[]{:S(2)}) collective-permute-start(bf16[128,640]{1,0:T(8,128)(2,1)} %bitcast.14), channel_id=1, source_target_pairs={{0,56},{4,60},{8,32},{12,36},{16,40},{20,44},{24,48},{28,52},{32,2... | collective-permute-start | bytes 491528 | tf_op jit(solution)/shard_map/ppermute | solution.py:215
  4.6 8.9 %collective-permute-start.12 = (bf16[128,640]{1,0:T(8,128)(2,1)}, bf16[128,640]{1,0:T(8,128)(2,1)S(1)}, u32[]{:S(2)}, u32[]{:S(2)}) collective-permute-start(bf16[128,640]{1,0:T(8,128)(2,1)} %bitcast.15), channel_id=1, source_target_pairs={{0,16},{4,20},{8,24},{12,28},{16,0},{20,4},{24,8},{28,12},{32,48},... | collective-permute-start | bytes 491528 | tf_op jit(solution)/shard_map/ppermute | solution.py:215
  9.9 7.9 %collective-permute-start.13 = (bf16[128,640]{1,0:T(8,128)(2,1)}, bf16[128,640]{1,0:T(8,128)(2,1)S(1)}, u32[]{:S(2)}, u32[]{:S(2)}) collective-permute-start(bf16[128,640]{1,0:T(8,128)(2,1)} %bitcast.16), channel_id=1, source_target_pairs={{0,48},{4,52},{8,56},{12,60},{16,32},{20,36},{24,40},{28,44},{32,1... | collective-permute-start | bytes 491528 | tf_op jit(solution)/shard_map/ppermute | solution.py:215
  12.3 5.6 %collective-permute-start.3 = (bf16[128,640]{1,0:T(8,128)(2,1)}, bf16[128,640]{1,0:T(8,128)(2,1)S(1)}, u32[]{:S(2)}, u32[]{:S(2)}) collective-permute-start(bf16[128,640]{1,0:T(8,128)(2,1)} %bitcast.21), channel_id=1, source_target_pairs={{0,4},{4,0},{8,12},{12,8},{16,20},{20,16},{24,28},{28,24},{32,36},... | collective-permute-start | bytes 491528 | tf_op jit(solution)/shard_map/ppermute | solution.py:217
  13.5 6.0 %collective-permute-start.5 = (bf16[128,640]{1,0:T(8,128)(2,1)}, bf16[128,640]{1,0:T(8,128)(2,1)S(1)}, u32[]{:S(2)}, u32[]{:S(2)}) collective-permute-start(bf16[128,640]{1,0:T(8,128)(2,1)} %bitcast.24), channel_id=1, source_target_pairs={{0,4},{4,0},{8,12},{12,8},{16,20},{20,16},{24,28},{28,24},{32,36},... | collective-permute-start | bytes 491528 | tf_op jit(solution)/shard_map/ppermute | solution.py:217
  17.8 19.2 %collective-permute-start = (bf16[128,640]{1,0:T(8,128)(2,1)}, bf16[128,640]{1,0:T(8,128)(2,1)S(1)}, u32[]{:S(2)}, u32[]{:S(2)}) collective-permute-start(bf16[128,640]{1,0:T(8,128)(2,1)} %bitcast.17), channel_id=1, source_target_pairs={{0,32},{4,36},{8,40},{12,44},{16,48},{20,52},{24,56},{28,60},{32,0... | collective-permute-start | bytes 491528 | tf_op jit(solution)/shard_map/ppermute | solution.py:215
  17.9 20.0 %collective-permute-start.1 = (bf16[128,640]{1,0:T(8,128)(2,1)}, bf16[128,640]{1,0:T(8,128)(2,1)S(1)}, u32[]{:S(2)}, u32[]{:S(2)}) collective-permute-start(bf16[128,640]{1,0:T(8,128)(2,1)} %bitcast.18), channel_id=1, source_target_pairs={{0,8},{4,12},{8,16},{12,20},{16,24},{20,28},{24,0},{28,4},{32,40},... | collective-permute-start | bytes 491528 | tf_op jit(solution)/shard_map/ppermute | solution.py:215
  19.5 21.5 %collective-permute-start.2 = (bf16[128,640]{1,0:T(8,128)(2,1)}, bf16[128,640]{1,0:T(8,128)(2,1)S(1)}, u32[]{:S(2)}, u32[]{:S(2)}) collective-permute-start(bf16[128,640]{1,0:T(8,128)(2,1)} %bitcast.19), channel_id=1, source_target_pairs={{0,24},{4,28},{8,0},{12,4},{16,8},{20,12},{24,16},{28,20},{32,56},... | collective-permute-start | bytes 491528 | tf_op jit(solution)/shard_map/ppermute | solution.py:215
  22.1 0.7 copy-start.3
  22.8 1.1 copy-start.7
  23.8 1.1 copy-start.9
  24.9 0.9 copy-start.12
  25.8 0.9 copy-start.14
  26.8 0.7 copy-start.16
  27.4 34.6 %copy-start = (bf16[640,5120]{1,0:T(8,128)(2,1)S(1)}, bf16[640,5120]{1,0:T(8,128)(2,1)}, u32[]{:S(2)}) copy-start(bf16[640,5120]{1,0:T(8,128)(2,1)} %refs_8_.1) | copy-start | bytes 19660804
  34.0 19.6 %collective-permute-start.14 = (bf16[656,128]{1,0:T(8,128)(2,1)S(1)}, bf16[656,128]{1,0:T(8,128)(2,1)S(1)}, u32[]{:S(2)}, u32[]{:S(2)}) collective-permute-start(bf16[656,128]{1,0:T(8,128)(2,1)S(1)} %get-tuple-element.21), channel_id=1, source_target_pairs={{0,56},{4,60},{8,32},{12,36},{16,40},{20,44},{24,48},{28,52},{32,2... | collective-permute-start | bytes 503816 | tf_op jit(solution)/shard_map/ppermute | solution.py:223
  36.0 19.4 %collective-permute-start.15 = (bf16[656,128]{1,0:T(8,128)(2,1)S(1)}, bf16[656,128]{1,0:T(8,128)(2,1)S(1)}, u32[]{:S(2)}, u32[]{:S(2)}) collective-permute-start(bf16[656,128]{1,0:T(8,128)(2,1)S(1)} %get-tuple-element.22), channel_id=1, source_target_pairs={{0,40},{4,44},{8,48},{12,52},{16,56},{20,60},{24,32},{28,36},{32,8... | collective-permute-start | bytes 503816 | tf_op jit(solution)/shard_map/ppermute | solution.py:223
  37.0 18.6 %collective-permute-start.16 = (bf16[656,128]{1,0:T(8,128)(2,1)S(1)}, bf16[656,128]{1,0:T(8,128)(2,1)S(1)}, u32[]{:S(2)}, u32[]{:S(2)}) collective-permute-start(bf16[656,128]{1,0:T(8,128)(2,1)S(1)} %get-tuple-element.23), channel_id=1, source_target_pairs={{0,16},{4,20},{8,24},{12,28},{16,0},{20,4},{24,8},{28,12},{32,48},... | collective-permute-start | bytes 503816 | tf_op jit(solution)/shard_map/ppermute | solution.py:223
  37.9 17.8 %collective-permute-start.17 = (bf16[656,128]{1,0:T(8,128)(2,1)S(1)}, bf16[656,128]{1,0:T(8,128)(2,1)S(1)}, u32[]{:S(2)}, u32[]{:S(2)}) collective-permute-start(bf16[656,128]{1,0:T(8,128)(2,1)S(1)} %get-tuple-element.24), channel_id=1, source_target_pairs={{0,48},{4,52},{8,56},{12,60},{16,32},{20,36},{24,40},{28,44},{32,1... | collective-permute-start | bytes 503816 | tf_op jit(solution)/shard_map/ppermute | solution.py:223
  41.0 1.1 copy-start.8
  42.1 1.1 copy-start.10
  43.2 0.9 copy-start.11
  44.1 0.9 copy-start.13
  45.0 0.9 copy-start.15
  52.6 5.4 %collective-permute-start.7 = (bf16[656,128]{1,0:T(8,128)(2,1)S(1)}, bf16[656,128]{1,0:T(8,128)(2,1)S(1)}, u32[]{:S(2)}, u32[]{:S(2)}) collective-permute-start(bf16[656,128]{1,0:T(8,128)(2,1)S(1)} %get-tuple-element.18), channel_id=1, source_target_pairs={{0,32},{4,36},{8,40},{12,44},{16,48},{20,52},{24,56},{28,60},{32,0... | collective-permute-start | bytes 503816 | tf_op jit(solution)/shard_map/ppermute | solution.py:223
  53.7 5.4 %collective-permute-start.8 = (bf16[656,128]{1,0:T(8,128)(2,1)S(1)}, bf16[656,128]{1,0:T(8,128)(2,1)S(1)}, u32[]{:S(2)}, u32[]{:S(2)}) collective-permute-start(bf16[656,128]{1,0:T(8,128)(2,1)S(1)} %get-tuple-element.19), channel_id=1, source_target_pairs={{0,24},{4,28},{8,0},{12,4},{16,8},{20,12},{24,16},{28,20},{32,56},... | collective-permute-start | bytes 503816 | tf_op jit(solution)/shard_map/ppermute | solution.py:223
  55.4 6.6 %collective-permute-start.9 = (bf16[656,128]{1,0:T(8,128)(2,1)S(1)}, bf16[656,128]{1,0:T(8,128)(2,1)S(1)}, u32[]{:S(2)}, u32[]{:S(2)}) collective-permute-start(bf16[656,128]{1,0:T(8,128)(2,1)S(1)} %get-tuple-element.20), channel_id=1, source_target_pairs={{0,8},{4,12},{8,16},{12,20},{16,24},{20,28},{24,0},{28,4},{32,40},... | collective-permute-start | bytes 503816 | tf_op jit(solution)/shard_map/ppermute | solution.py:223
  67.7 36.7 %copy-start.1 = (f32[32,2,5120]{2,1,0:T(2,128)S(1)}, f32[32,2,5120]{2,1,0:T(2,128)}, u32[]{:S(2)}) copy-start(f32[32,2,5120]{2,1,0:T(2,128)} %table.1) | copy-start | bytes 3932164
  67.7 36.7 %copy-start.2 = (bf16[1,32,5120]{2,1,0:T(8,128)(2,1)S(1)}, bf16[1,32,5120]{2,1,0:T(8,128)(2,1)}, u32[]{:S(2)}) copy-start(bf16[1,32,5120]{2,1,0:T(8,128)(2,1)} %param.22) | copy-start | bytes 983044
  67.7 36.7 %copy-start.4 = (s32[4]{0:T(128)S(1)}, s32[4]{0:T(128)}, u32[]{:S(2)}) copy-start(s32[4]{0:T(128)} %group_branch.5) | copy-start | bytes 52
  67.7 36.7 %copy-start.5 = (f32[4]{0:T(128)S(1)}, f32[4]{0:T(128)}, u32[]{:S(2)}) copy-start(f32[4]{0:T(128)} %guidance_w.1) | copy-start | bytes 52
  67.7 36.7 %copy-start.6 = (s32[32]{0:T(128)S(1)}, s32[32]{0:T(128)}, u32[]{:S(2)}) copy-start(s32[32]{0:T(128)} %frame_level.1) | copy-start | bytes 388
  67.7 26.7 %collective-permute-start.18 = (bf16[32,5120]{1,0:T(8,128)(2,1)}, bf16[32,5120]{1,0:T(8,128)(2,1)}, u32[]{:S(2)}, u32[]{:S(2)}) collective-permute-start(bf16[32,5120]{1,0:T(8,128)(2,1)} %get-tuple-element.26), channel_id=1, source_target_pairs={{0,1},{1,2},{2,3},{3,0},{4,5},{5,6},{6,7},{7,4},{8,9},{9,10},{10,1... | collective-permute-start | bytes 983048 | tf_op jit(solution)/shard_map/ppermute | solution.py:227
  71.3 23.1 %collective-permute-start.19 = (bf16[32,5120]{1,0:T(8,128)(2,1)}, bf16[32,5120]{1,0:T(8,128)(2,1)}, u32[]{:S(2)}, u32[]{:S(2)}) collective-permute-start(bf16[32,5120]{1,0:T(8,128)(2,1)} %get-tuple-element.27), channel_id=1, source_target_pairs={{0,3},{1,0},{2,1},{3,2},{4,7},{5,4},{6,5},{7,6},{8,11},{9,8},{10,9... | collective-permute-start | bytes 983048 | tf_op jit(solution)/shard_map/ppermute | solution.py:227
  74.4 29.9 %collective-permute-start.20 = (bf16[32,5120]{1,0:T(8,128)(2,1)}, bf16[32,5120]{1,0:T(8,128)(2,1)}, u32[]{:S(2)}, u32[]{:S(2)}) collective-permute-start(bf16[32,5120]{1,0:T(8,128)(2,1)} %get-tuple-element.28), channel_id=1, source_target_pairs={{0,2},{1,3},{2,0},{3,1},{4,6},{5,7},{6,4},{7,5},{8,10},{9,11},{10,... | collective-permute-start | bytes 983048 | tf_op jit(solution)/shard_map/ppermute | solution.py:227
  106.5 5.3 %collective-permute-start.21 = (f32[32,64]{1,0:T(8,128)S(1)}, f32[32,64]{1,0:T(8,128)S(1)}, u32[]{:S(2)}, u32[]{:S(2)}) collective-permute-start(f32[32,64]{1,0:T(8,128)S(1)} %head.1), channel_id=1, source_target_pairs={{0,128},{64,192},{128,0},{192,64},{1,129},{65,193},{129,1},{193,65... | collective-permute-start | bytes 24584 | tf_op jit(solution)/shard_map/ppermute | solution.py:231
  107.8 4.0 %collective-permute-start.22 = (f32[32,64]{1,0:T(8,128)S(1)}, f32[32,64]{1,0:T(8,128)S(1)}, u32[]{:S(2)}, u32[]{:S(2)}) collective-permute-start(f32[32,64]{1,0:T(8,128)S(1)} %head.1), channel_id=1, source_target_pairs={{0,64},{64,128},{128,192},{192,0},{1,65},{65,129},{129,193},{193,1... | collective-permute-start | bytes 24584 | tf_op jit(solution)/shard_map/ppermute | solution.py:231
  110.0 4.9 %collective-permute-start.23 = (f32[32,64]{1,0:T(8,128)S(1)}, f32[32,64]{1,0:T(8,128)S(1)}, u32[]{:S(2)}, u32[]{:S(2)}) collective-permute-start(f32[32,64]{1,0:T(8,128)S(1)} %head.1), channel_id=1, source_target_pairs={{0,192},{64,0},{128,64},{192,128},{1,193},{65,1},{129,65},{193,129... | collective-permute-start | bytes 24584 | tf_op jit(solution)/shard_map/ppermute | solution.py:231

commit v2 on v1

v2 whole, which is shorter than its diff:
```python
import functools

import jax
import jax.numpy as jnp
from jax import lax
from jax.experimental import pallas as pl
from jax.experimental.pallas import tpu as pltpu
from jax.sharding import PartitionSpec as P

HSZ = 128
FRAME_TOK = 64
NEG = -1e30
LANES = 128
STAT_ROWS = 16
SCORE_TO_EXP2 = HSZ ** (-0.5) * 1.4426950408889634

XS = 4
MPS = 4


def hop(dz, dx, dc):
    return [
        ((z * XS + x) * 2 + c, ((z ^ dz) * XS + (x + dx) % XS) * 2 + (c ^ dc))
        for z in range(2)
        for x in range(XS)
        for c in range(2)
    ]


def pair_hop(place):
    pairs = []
    for z in range(2):
        for m in range(MPS):
            to_z, to_m = place(z, m)
            for r in range(XS * 2):
                pairs.append(
                    ((z * XS * 2 + r) * MPS + m, (to_z * XS * 2 + r) * MPS + to_m % MPS)
                )
    return pairs


def onward(z, m):
    return z, m + 2 * z - 1


def across_onward(z, m):
    return 1 - z, m + 2 * z - 1


def turn(step, count=4):
    return [(i, (i + step) % count) for i in range(count)]


def join_kernel(here, there, out):
    step = here.shape[0] // MPS
    mine = lax.axis_index("mp")
    side = lax.axis_index("seq") // (XS * 2)
    at = 0
    for first, second, toward in ((there, here, 3 - 2 * side), (here, there, 1 + 2 * side)):
        for ref, k in ((first, toward), (first, 2), (second, toward), (second, 0)):
            start = pl.multiple_of(lax.rem(mine + k, MPS) * step, step)
            out[at : at + step, :] = ref[pl.ds(start, step), :]
            at += step


def join(here, there):
    rows, feat = here.shape
    vmem = pl.BlockSpec(memory_space=pltpu.VMEM)
    return pl.pallas_call(
        join_kernel,
        out_shape=jax.ShapeDtypeStruct((2 * rows, feat), here.dtype),
        in_specs=[vmem] * 2,
        out_specs=vmem,
        compiler_params=pltpu.CompilerParams(vmem_limit_bytes=4 * 2**20),
        name="join",
    )(here, there)


def pack_kernel(
    span_q,
    span_k,
    span_v,
    hist_k,
    hist_v,
    hist_len,
    group_branch,
    out,
    bias,
    held,
    near_v,
    far_v,
    lens,
    order,
    sems,
):
    near, feat = span_k.shape
    far = hist_k.shape[0]
    count = near + far
    fetches = [
        pltpu.make_async_copy(source, target, sems.at[i])
        for i, (source, target) in enumerate(
            (
                (span_v, near_v),
                (hist_v, far_v),
                (span_k, out.at[:near]),
                (hist_k, out.at[near:count]),
                (hist_len, lens),
                (group_branch, order),
                (span_q, held),
            )
        )
    ]
    for fetch in fetches:
        fetch.start()
    fetches[0].wait()
    out[count:, :near] = near_v[...].T
    fetches[1].wait()
    out[count:, near:] = far_v[...].T
    for fetch in fetches[2:]:
        fetch.wait()
    length = lens[order[lax.axis_index("branch")]]
    seq = lax.axis_index("seq")
    lanes = bias.shape[1]
    for i, place in enumerate((seq, seq + 1 - 2 * lax.rem(seq, 2))):
        spot = place * far + lax.broadcasted_iota(jnp.int32, (far, lanes), 0)
        bias[i * count : i * count + near, :] = jnp.zeros((near, lanes), jnp.float32)
        bias[i * count + near : (i + 1) * count, :] = jnp.where(spot < length, 0.0, NEG)


def pack(span_q, span_k, span_v, hist_k, hist_v, hist_len, group_branch):
    near, feat = span_k.shape
    far = hist_k.shape[0]
    count = near + far
    vmem = pl.BlockSpec(memory_space=pltpu.VMEM)
    return pl.pallas_call(
        pack_kernel,
        out_shape=[
            jax.ShapeDtypeStruct((count + feat, feat), span_k.dtype),
            jax.ShapeDtypeStruct((2 * count, LANES), jnp.float32),
            jax.ShapeDtypeStruct(span_q.shape, span_q.dtype),
        ],
        in_specs=[pl.BlockSpec(memory_space=pltpu.HBM)] * 7,
        out_specs=[vmem] * 3,
        scratch_shapes=[
            pltpu.VMEM((near, feat), span_v.dtype),
            pltpu.VMEM((far, feat), hist_v.dtype),
            pltpu.SMEM(hist_len.shape, jnp.int32),
            pltpu.SMEM(group_branch.shape, jnp.int32),
            pltpu.SemaphoreType.DMA((7,)),
        ],
        compiler_params=pltpu.CompilerParams(vmem_limit_bytes=8 * 2**20),
        cost_estimate=pl.CostEstimate(flops=6 * 10**9, bytes_accessed=4 * count * feat, transcendentals=0),
        name="pack",
    )(
        *[
            pltpu.with_memory_space_constraint(a, pltpu.HBM)
            for a in (span_q, span_k, span_v, hist_k, hist_v, hist_len, group_branch)
        ]
    )


def attend_kernel(queries, mine_pack, core_pack, bias, *rest):
    sent = rest[-1]
    packs = (mine_pack, core_pack)
    feat = queries.shape[1]
    rows = queries.shape[0] // 2
    heads = feat // HSZ
    count = mine_pack.shape[0] - feat
    levels = []
    for h in range(heads):
        cols = slice(h * HSZ, (h + 1) * HSZ)
        q = queries[:, cols]
        scores = []
        for i, pack_ref in enumerate(packs):
            s = lax.dot_general(
                pack_ref[:count, cols],
                q,
                (((1,), (1,)), ((), ())),
                preferred_element_type=jnp.float32,
            )
            offset = bias[i * count : (i + 1) * count, :]
            scores.append(s + jnp.concatenate([offset] * (s.shape[1] // LANES), axis=1))
        peak = functools.reduce(jnp.maximum, [jnp.max(s, axis=0, keepdims=True) for s in scores])
        total, summed = 0.0, 0.0
        for pack_ref, s in zip(packs, scores):
            weights = jnp.exp2((s - peak) * SCORE_TO_EXP2)
            total = total + jnp.sum(weights, axis=0, keepdims=True)
            summed = summed + jnp.dot(
                pack_ref[count + h * HSZ : count + (h + 1) * HSZ, :],
                weights.astype(jnp.bfloat16),
                preferred_element_type=jnp.float32,
            )
        out = (summed / total).astype(jnp.bfloat16)
        for i in range(2):
            start = i * (feat + STAT_ROWS) + h * HSZ
            sent[start : start + HSZ, :] = out[:, i * rows : (i + 1) * rows]
        levels.append(peak * SCORE_TO_EXP2 + jnp.log2(total))
    stats = stat_rows(levels)
    for i in range(2):
        start = i * (feat + STAT_ROWS) + feat
        sent[start : start + STAT_ROWS, :] = stats[:, i * rows : (i + 1) * rows]


def stat_rows(levels):
    level = jnp.concatenate(levels, axis=0)
    high = level.astype(jnp.bfloat16).astype(jnp.float32)
    middle = (level - high).astype(jnp.bfloat16).astype(jnp.float32)
    spare = jnp.zeros((STAT_ROWS - 3 * level.shape[0], level.shape[1]), jnp.float32)
    return jnp.concatenate([high, middle, level - high - middle, spare], axis=0).astype(jnp.bfloat16)


def attend(queries, packs, bias, after):
    rows, feat = queries.shape[0] // 2, queries.shape[1]
    count = packs[0].shape[0] - feat
    vmem = pl.BlockSpec(memory_space=pltpu.VMEM)
    return pl.pallas_call(
        attend_kernel,
        out_shape=jax.ShapeDtypeStruct((2 * (feat + STAT_ROWS), rows), jnp.bfloat16),
        in_specs=[vmem] * 4 + [pl.BlockSpec(memory_space=pl.ANY)] * len(after),
        out_specs=vmem,
        compiler_params=pltpu.CompilerParams(vmem_limit_bytes=16 * 2**20),
        cost_estimate=pl.CostEstimate(
            flops=16 * rows * count * feat,
            bytes_accessed=8 * count * feat,
            transcendentals=4 * rows * count * (feat // HSZ),
        ),
        name="attend",
    )(queries, *packs, bias, *after)


def merged(parts, heads):
    feat = heads * HSZ
    levels = []
    for ref, at in parts:
        s = ref[at + feat : at + feat + STAT_ROWS, :].astype(jnp.float32)
        levels.append(s[:heads] + s[heads : 2 * heads] + s[2 * heads : 3 * heads])
    peak = functools.reduce(jnp.maximum, levels)
    shares = [jnp.exp2(level - peak) for level in levels]
    total = functools.reduce(jnp.add, shares)
    over = 1.0 / total
    shares = [share * over for share in shares]
    sums = [
        functools.reduce(
            jnp.add,
            [
                ref[at + h * HSZ : at + (h + 1) * HSZ, :].astype(jnp.float32) * share[h : h + 1]
                for (ref, at), share in zip(parts, shares)
            ],
        )
        for h in range(heads)
    ]
    return sums, peak + jnp.log2(total)


def merge_kernel(*refs):
    out = refs[-1]
    feat = out.shape[0] - STAT_ROWS
    sums, level = merged([(ref, out.shape[0]) for ref in refs[:-1]], feat // HSZ)
    for h, summed in enumerate(sums):
        out[h * HSZ : (h + 1) * HSZ, :] = summed.astype(jnp.bfloat16)
    out[feat:, :] = stat_rows([level])


def merge(parts):
    height, rows = parts[0].shape
    vmem = pl.BlockSpec(memory_space=pltpu.VMEM)
    return pl.pallas_call(
        merge_kernel,
        out_shape=jax.ShapeDtypeStruct((height // 2, rows), jnp.bfloat16),
        in_specs=[vmem] * len(parts),
        out_specs=vmem,
        compiler_params=pltpu.CompilerParams(vmem_limit_bytes=4 * 2**20),
        name="merge",
    )(*parts)


def project_kernel(count, *refs):
    parts = refs[:count]
    weight = refs[count]
    outs = refs[count + 1 : count + 1 + MPS]
    held = refs[count + 1 + MPS]
    feat, width = weight.shape
    for h, summed in enumerate(merged([(part, 0) for part in parts], feat // HSZ)[0]):
        held[:, h * HSZ : (h + 1) * HSZ] = summed.T.astype(jnp.bfloat16)
    step = outs[0].shape[0]
    chunk = 512
    for first in range(0, width, chunk):
        cols = slice(first, first + chunk)
        product = jnp.dot(held[...], weight[:, cols], preferred_element_type=jnp.float32)
        for i, out in enumerate(outs):
            out[:, cols] = product[i * step : (i + 1) * step].astype(out.dtype)


def project(parts, weight):
    feat, width = weight.shape
    rows = parts[0].shape[1]
    vmem = pl.BlockSpec(memory_space=pltpu.VMEM)
    return pl.pallas_call(
        functools.partial(project_kernel, len(parts)),
        out_shape=[jax.ShapeDtypeStruct((rows // MPS, width), jnp.bfloat16)] * MPS,
        in_specs=[vmem] * (len(parts) + 1),
        out_specs=[vmem] * MPS,
        scratch_shapes=[pltpu.VMEM((rows, feat), jnp.bfloat16)],
        compiler_params=pltpu.CompilerParams(vmem_limit_bytes=24 * 2**20),
        cost_estimate=pl.CostEstimate(
            flops=2 * rows * feat * width, bytes_accessed=2 * feat * width, transcendentals=0
        ),
        name="project",
    )(*parts, weight)


def head_kernel(
    group_branch, guidance_w, frame_level, p0, p1, p2, residual, table, weight, out, held, sem
):
    rows, width = residual.shape
    token = (lax.axis_index("seq") * 4 + lax.axis_index("mp")) * rows
    level = frame_level[token // FRAME_TOK]
    fetch = pltpu.make_async_copy(table.at[level], held, sem)
    fetch.start()
    stream = residual[...].astype(jnp.float32) + (
        (p0[...].astype(jnp.float32) + p1[...].astype(jnp.float32)) + p2[...].astype(jnp.float32)
    )
    mean = jnp.mean(stream, axis=1, keepdims=True)
    centred = stream - mean
    variance = jnp.mean(centred * centred, axis=1, keepdims=True)
    normed = centred * lax.rsqrt(variance + 1e-06)
    fetch.wait()
    modulated = (normed * (1.0 + held[1:2, :]) + held[0:1, :]).astype(jnp.bfloat16)
    velocity = jnp.dot(modulated, weight[...], preferred_element_type=jnp.float32)
    out[...] = velocity * guidance_w[group_branch[lax.axis_index("branch")]]


def head(group_branch, guidance_w, frame_level, parts, residual, table, weight):
    rows, width = residual.shape
    vmem = pl.BlockSpec(memory_space=pltpu.VMEM)
    smem = pl.BlockSpec(memory_space=pltpu.SMEM)
    return pl.pallas_call(
        head_kernel,
        out_shape=jax.ShapeDtypeStruct((rows, weight.shape[1]), jnp.float32),
        in_specs=[smem] * 3 + [vmem] * 4 + [pl.BlockSpec(memory_space=pl.ANY), vmem],
        out_specs=vmem,
        scratch_shapes=[pltpu.VMEM(table.shape[1:], jnp.float32), pltpu.SemaphoreType.DMA],
        compiler_params=pltpu.CompilerParams(vmem_limit_bytes=24 * 2**20),
        name="head",
    )(group_branch, guidance_w, frame_level, *parts, residual, table, weight)


def body(
    span_q,
    span_k,
    span_v,
    hist_k,
    hist_v,
    hist_len,
    group_branch,
    guidance_w,
    frame_level,
    residual,
    out_weight,
    mod_table,
    head_weight,
):
    mine = span_q[0]
    across = lax.ppermute(mine, "seq", hop(1, 0, 0))
    own, bias, held = pack(mine, span_k[0], span_v[0], hist_k[0], hist_v[0], hist_len, group_branch)
    packs = [own, lax.ppermute(own, "seq", hop(0, 0, 1))]
    pairs = {0: join(held, across)}
    for dx in (1, 3, 2):
        pairs[dx] = lax.ppermute(pairs[0], "seq", hop(0, dx, 0))
    parts = []
    made = []
    for dx in (0, 1, 3, 2):
        sent = attend(pairs[dx], packs, bias, made[-1:])
        made.append(sent)
        parts.append(lax.ppermute(sent, "seq", hop(0, -dx, 0)) if dx else sent)
    parts.append(lax.ppermute(merge(parts), "seq", hop(1, 0, 0)))
    near_block, far_block, side_block, own_block = project(parts, out_weight)
    passed = lax.ppermute(far_block, ("seq", "mp"), pair_hop(onward))
    aside = lax.ppermute(side_block, ("seq", "mp"), pair_hop(onward))
    joined = (near_block.astype(jnp.float32) + passed.astype(jnp.float32)).astype(jnp.bfloat16)
    reduced = [own_block, aside, lax.ppermute(joined, ("seq", "mp"), pair_hop(across_onward))]
    velocity = head(
        group_branch, guidance_w, frame_level, reduced, residual[0], mod_table, head_weight
    )
    around = [lax.ppermute(velocity, "branch", turn(k)) for k in (1, 3, 2)]
    return (velocity + around[2]) + (around[0] + around[1])


def solution(mesh):
    in_specs = (
        P("branch", "seq", "mp"),
        P("branch", "seq", "mp"),
        P("branch", "seq", "mp"),
        P("branch", "seq", "mp"),
        P("branch", "seq", "mp"),
        P(),
        P(),
        P(),
        P(),
        P("branch", ("seq", "mp"), None),
        P("mp", None),
        P(),
        P(),
    )
    out_specs = P(("seq", "mp"), None)
    return jax.shard_map(body, mesh=mesh, in_specs=in_specs, out_specs=out_specs, check_vma=False)
```

time: 116 us -> 93.7 us (0.81)
  the two profiles are of different devices: /device:TPU:56 before, /device:TPU:24 now
where the time goes in v2:
time: 93.7 us; the launch traced here: 93.6 us
  waiting for transfers between devices  44 us (47%)
  starting transfers between devices  26.8 us (29%)
  Pallas kernels  19.5 us (21%)
  local copies, waits for them, and re-layouts  1.69 us (2%)
  other arithmetic  1.42 us (2%)
    pallas_call x4, Pallas kernels, attend(): pl.pallas_call(attend_kernel, out_shape=jax.ShapeDtypeStruct((2 * (feat +...  13.7 us
    ppermute x3, waiting for transfers between devices, body(): parts.append(lax.ppermute(sent, 'seq', hop(0, -dx, 0)) if dx else sent)  11.2 us
    ppermute x1, waiting for transfers between devices, body(): passed = lax.ppermute(far_block, ('seq', 'mp'), pair_hop(onward))  6.7 us
    ppermute x1, starting transfers between devices, body(): passed = lax.ppermute(far_block, ('seq', 'mp'), pair_hop(onward))  5.61 us
    ppermute x3, starting transfers between devices, body(): pairs[dx] = lax.ppermute(pairs[0], 'seq', hop(0, dx, 0))  5.13 us
    ppermute x3, waiting for transfers between devices, body(): pairs[dx] = lax.ppermute(pairs[0], 'seq', hop(0, dx, 0))  5.11 us
    ppermute x3, waiting for transfers between devices, body(): around = [lax.ppermute(velocity, 'branch', turn(k)) for k in (1, 3, 2)]  4.95 us
    ppermute x1, waiting for transfers between devices, body(): lax.ppermute(joined, ('seq', 'mp'), pair_hop(across_onward))  4.93 us
  transfers between devices with their start and end apart: 15, of which 11 were waited for; matrix products, arithmetic and copies ran while one was open for 3% of the time, Pallas kernels for 11%

profile of v2, /device:TPU:24, one launch (start us, length us, event | category | flops | bytes accessed | tf_op | source)
XLA Modules:
  0.0 93.6 jit_solution(15786432350299312885)
XLA Ops:
  0.0 0.0 copy-start.5
  0.0 1.6 %pack.1 = (bf16[1280,640]{1,0:T(8,128)(2,1)S(1)}, f32[1280,128]{1,0:T(8,128)S(1)}, bf16[128,640]{1,0:T(8,128)(2,1)S(1)}) custom-call(bf16[128,640]{1,0:T(8,128)(2,1)} %bitcast.13, bf16[128,640]{1,0:T(8,128)(2,1)} %bitcast.11, bf16[128,640]{1,0:T(8,128)(2,1)} %bitcast.12, bf16[512,640]{1,0:T(8,128)(2,1)} %bitcast.9, bf16[512,640]{1,0:T(8,128)(2,1)} %bitcast.10, ...), custom_call_target="tpu_custom_call" | custom-call | flops 6000000000 | bytes 1638400 | tf_op jit(solution)/shard_map/pack/pallas_call | solution.py:135
  1.6 0.1 collective-permute-start.1
  1.7 0.0 copy-done.5
  1.7 2.0 %collective-permute-start = (bf16[128,640]{1,0:T(8,128)(2,1)S(1)}, bf16[128,640]{1,0:T(8,128)(2,1)S(1)}, u32[]{:S(2)}, u32[]{:S(2)}) collective-permute-start(bf16[128,640]{1,0:T(8,128)(2,1)S(1)} %bitcast.14), channel_id=1, source_target_pairs={{0,32},{4,36},{8,40},{12,44},{16,48},{20,52},{24,56},{28,60},{32,0... | collective-permute-start | bytes 491528 | tf_op jit(solution)/shard_map/ppermute | solution.py:364
  3.7 4.8 %collective-permute-done.there = bf16[128,640]{1,0:T(8,128)(2,1)S(1)} collective-permute-done((bf16[128,640]{1,0:T(8,128)(2,1)S(1)}, bf16[128,640]{1,0:T(8,128)(2,1)S(1)}, u32[]{:S(2)}, u32[]{:S(2)}) %collective-permute-start) | collective-permute-done | bytes 163872 | tf_op jit(solution)/shard_map/ppermute | solution.py:364
  8.5 1.6 %collective-permute-start.2 = (bf16[256,640]{1,0:T(8,128)(2,1)S(1)}, bf16[256,640]{1,0:T(8,128)(2,1)S(1)}, u32[]{:S(2)}, u32[]{:S(2)}) collective-permute-start(bf16[256,640]{1,0:T(8,128)(2,1)S(1)} %join.1.queries), channel_id=1, source_target_pairs={{0,8},{4,12},{8,16},{12,20},{16,24},{20,28},{24,0},{28,4},{32,40},... | collective-permute-start | bytes 983048 | tf_op jit(solution)/shard_map/ppermute | solution.py:369
  10.1 1.7 %collective-permute-start.4 = (bf16[256,640]{1,0:T(8,128)(2,1)S(1)}, bf16[256,640]{1,0:T(8,128)(2,1)S(1)}, u32[]{:S(2)}, u32[]{:S(2)}) collective-permute-start(bf16[256,640]{1,0:T(8,128)(2,1)S(1)} %join.1.queries), channel_id=1, source_target_pairs={{0,24},{4,28},{8,0},{12,4},{16,8},{20,12},{24,16},{28,20},{32,56},... | collective-permute-start | bytes 983048 | tf_op jit(solution)/shard_map/ppermute | solution.py:369
  11.8 1.8 %collective-permute-start.6 = (bf16[256,640]{1,0:T(8,128)(2,1)S(1)}, bf16[256,640]{1,0:T(8,128)(2,1)S(1)}, u32[]{:S(2)}, u32[]{:S(2)}) collective-permute-start(bf16[256,640]{1,0:T(8,128)(2,1)S(1)} %join.1.queries), channel_id=1, source_target_pairs={{0,16},{4,20},{8,24},{12,28},{16,0},{20,4},{24,8},{28,12},{32,48},... | collective-permute-start | bytes 983048 | tf_op jit(solution)/shard_map/ppermute | solution.py:369
  13.7 0.0 collective-permute-done.1.core_pack
  13.7 3.4 %attend.4.rest_0_.refs_0_ = bf16[1312,128]{1,0:T(8,128)(2,1)S(1)} custom-call(bf16[256,640]{1,0:T(8,128)(2,1)S(1)} %join.1.queries, bf16[1280,640]{1,0:T(8,128)(2,1)S(1)} %get-tuple-element.13.mine_pack, bf16[1280,640]{1,0:T(8,128)(2,1)S(1)} %collective-permute-done.1.core_pack, f32[1280,128]{1,0:T(8,128)S(1)} %get-tuple-element.14.bias), custom_call_target="tpu_custom_call" | custom-call | flops 838860800 | bytes 3276800 | tf_op jit(solution)/shard_map/attend/pallas_call | solution.py:216
  17.0 2.4 %collective-permute-done.2.queries = bf16[256,640]{1,0:T(8,128)(2,1)S(1)} collective-permute-done((bf16[256,640]{1,0:T(8,128)(2,1)S(1)}, bf16[256,640]{1,0:T(8,128)(2,1)S(1)}, u32[]{:S(2)}, u32[]{:S(2)}) %collective-permute-start.2) | collective-permute-done | bytes 327712 | tf_op jit(solution)/shard_map/ppermute | solution.py:369
  19.4 0.0 slice-start
  19.4 3.4 %attend.5.rest_0_ = bf16[1312,128]{1,0:T(8,128)(2,1)S(1)} custom-call(bf16[256,640]{1,0:T(8,128)(2,1)S(1)} %collective-permute-done.2.queries, bf16[1280,640]{1,0:T(8,128)(2,1)S(1)} %get-tuple-element.13.mine_pack, bf16[1280,640]{1,0:T(8,128)(2,1)S(1)} %collective-permute-done.1.core_pack, f32[1280,128]{1,0:T(8,128)S(1)} %get-tuple-element.14.bias, ...), custom_call_target="tpu_custom_call" | custom-call | flops 838860800 | bytes 3276800 | tf_op jit(solution)/shard_map/attend/pallas_call | solution.py:216
  22.8 0.0 slice-start.1
  22.8 2.7 %collective-permute-done.4.queries = bf16[256,640]{1,0:T(8,128)(2,1)S(1)} collective-permute-done((bf16[256,640]{1,0:T(8,128)(2,1)S(1)}, bf16[256,640]{1,0:T(8,128)(2,1)S(1)}, u32[]{:S(2)}, u32[]{:S(2)}) %collective-permute-start.4) | collective-permute-done | bytes 327712 | tf_op jit(solution)/shard_map/ppermute | solution.py:369
  25.6 3.4 %attend.6.rest_0_ = bf16[1312,128]{1,0:T(8,128)(2,1)S(1)} custom-call(bf16[256,640]{1,0:T(8,128)(2,1)S(1)} %collective-permute-done.4.queries, bf16[1280,640]{1,0:T(8,128)(2,1)S(1)} %get-tuple-element.13.mine_pack, bf16[1280,640]{1,0:T(8,128)(2,1)S(1)} %collective-permute-done.1.core_pack, f32[1280,128]{1,0:T(8,128)S(1)} %get-tuple-element.14.bias, ...), custom_call_target="tpu_custom_call" | custom-call | flops 838860800 | bytes 3276800 | tf_op jit(solution)/shard_map/attend/pallas_call | solution.py:216
  28.9 0.0 collective-permute-done.6.queries
  28.9 3.6 %attend.7 = bf16[1312,128]{1,0:T(8,128)(2,1)S(1)} custom-call(bf16[256,640]{1,0:T(8,128)(2,1)S(1)} %collective-permute-done.6.queries, bf16[1280,640]{1,0:T(8,128)(2,1)S(1)} %get-tuple-element.13.mine_pack, bf16[1280,640]{1,0:T(8,128)(2,1)S(1)} %collective-permute-done.1.core_pack, f32[1280,128]{1,0:T(8,128)S(1)} %get-tuple-element.14.bias, ...), custom_call_target="tpu_custom_call" | custom-call | flops 838860800 | bytes 3276800 | tf_op jit(solution)/shard_map/attend/pallas_call | solution.py:216
  32.6 0.2 collective-permute-start.7
  32.7 4.4 %collective-permute-start.5 = (bf16[1312,128]{1,0:T(8,128)(2,1)S(1)}, bf16[1312,128]{1,0:T(8,128)(2,1)S(1)}, u32[]{:S(2)}, u32[]{:S(2)}) collective-permute-start(bf16[1312,128]{1,0:T(8,128)(2,1)S(1)} %attend.6.rest_0_), channel_id=1, source_target_pairs={{0,8},{4,12},{8,16},{12,20},{16,24},{20,28},{24,0},{28,4},{32,40},... | collective-permute-start | bytes 1007624 | tf_op jit(solution)/shard_map/ppermute | solution.py:375
  37.2 0.0 collective-permute-start.3
  37.2 7.7 %collective-permute-done.7.refs_3_ = bf16[1312,128]{1,0:T(8,128)(2,1)S(1)} collective-permute-done((bf16[1312,128]{1,0:T(8,128)(2,1)S(1)}, bf16[1312,128]{1,0:T(8,128)(2,1)S(1)}, u32[]{:S(2)}, u32[]{:S(2)}) %collective-permute-start.7) | collective-permute-done | bytes 335904 | tf_op jit(solution)/shard_map/ppermute | solution.py:375
  44.8 3.5 %collective-permute-done.5.refs_2_ = bf16[1312,128]{1,0:T(8,128)(2,1)S(1)} collective-permute-done((bf16[1312,128]{1,0:T(8,128)(2,1)S(1)}, bf16[1312,128]{1,0:T(8,128)(2,1)S(1)}, u32[]{:S(2)}, u32[]{:S(2)}) %collective-permute-start.5) | collective-permute-done | bytes 335904 | tf_op jit(solution)/shard_map/ppermute | solution.py:375
  48.4 0.0 collective-permute-done.3.refs_1_
  48.4 0.2 merge.1
  48.5 1.5 %collective-permute-start.8 = (bf16[656,128]{1,0:T(8,128)(2,1)S(1)}, bf16[656,128]{1,0:T(8,128)(2,1)S(1)}, u32[]{:S(2)}, u32[]{:S(2)}) collective-permute-start(bf16[656,128]{1,0:T(8,128)(2,1)S(1)} %merge.1), channel_id=1, source_target_pairs={{0,32},{4,36},{8,40},{12,44},{16,48},{20,52},{24,56},{28,60},{32,0... | collective-permute-start | bytes 503816 | tf_op jit(solution)/shard_map/ppermute | solution.py:376
  50.0 4.6 %collective-permute-done.8.refs_4_ = bf16[656,128]{1,0:T(8,128)(2,1)S(1)} collective-permute-done((bf16[656,128]{1,0:T(8,128)(2,1)S(1)}, bf16[656,128]{1,0:T(8,128)(2,1)S(1)}, u32[]{:S(2)}, u32[]{:S(2)}) %collective-permute-start.8) | collective-permute-done | bytes 167968 | tf_op jit(solution)/shard_map/ppermute | solution.py:376
  54.6 0.0 slice-done
  54.6 0.0 slice-done.1
  54.6 2.1 %project.1 = (bf16[32,5120]{1,0:T(8,128)(2,1)S(1)}, bf16[32,5120]{1,0:T(8,128)(2,1)S(1)}, bf16[32,5120]{1,0:T(8,128)(2,1)}, bf16[32,5120]{1,0:T(8,128)(2,1)S(1)}) custom-call(bf16[1312,128]{1,0:T(8,128)(2,1)S(1)} %attend.4.rest_0_.refs_0_, bf16[1312,128]{1,0:T(8,128)(2,1)S(1)} %collective-permute-done.3.refs_1_, ...), custom_call_target="tpu_custom_call" | custom-call | flops 838860800 | bytes 6553600 | tf_op jit(solution)/shard_map/project/pallas_call | solution.py:298
  56.7 0.0 copy-start
  56.7 0.0 copy-start.1
  56.7 0.0 copy-start.2
  56.7 0.0 copy-start.3
  56.8 0.0 copy-start.4
  56.8 5.6 %collective-permute-start.10 = (bf16[32,5120]{1,0:T(8,128)(2,1)S(1)}, bf16[32,5120]{1,0:T(8,128)(2,1)S(1)}, u32[]{:S(2)}, u32[]{:S(2)}) collective-permute-start(bf16[32,5120]{1,0:T(8,128)(2,1)S(1)} %get-tuple-element.18), channel_id=1, source_target_pairs={{0,3},{4,7},{8,11},{12,15},{16,19},{20,23},{24,27},{28,31},{1,0},{... | collective-permute-start | bytes 983048 | tf_op jit(solution)/shard_map/ppermute | solution.py:378
  62.4 1.5 %collective-permute-start.9 = (bf16[32,5120]{1,0:T(8,128)(2,1)}, bf16[32,5120]{1,0:T(8,128)(2,1)}, u32[]{:S(2)}, u32[]{:S(2)}) collective-permute-start(bf16[32,5120]{1,0:T(8,128)(2,1)} %get-tuple-element.16), channel_id=1, source_target_pairs={{0,3},{4,7},{8,11},{12,15},{16,19},{20,23},{24,27},{28,31},{1,0},{... | collective-permute-start | bytes 983048 | tf_op jit(solution)/shard_map/ppermute | solution.py:379
  63.8 6.7 %collective-permute-done.10 = bf16[32,5120]{1,0:T(8,128)(2,1)S(1)} collective-permute-done((bf16[32,5120]{1,0:T(8,128)(2,1)S(1)}, bf16[32,5120]{1,0:T(8,128)(2,1)S(1)}, u32[]{:S(2)}, u32[]{:S(2)}) %collective-permute-start.10) | collective-permute-done | bytes 327712 | tf_op jit(solution)/shard_map/ppermute | solution.py:378
  70.5 0.8 add_convert_fusion
  71.3 2.9 %collective-permute-start.11 = (bf16[32,5120]{1,0:T(8,128)(2,1)}, bf16[32,5120]{1,0:T(8,128)(2,1)}, u32[]{:S(2)}, u32[]{:S(2)}) collective-permute-start(bf16[32,5120]{1,0:T(8,128)(2,1)} %add_convert_fusion), channel_id=1, source_target_pairs={{0,35},{4,39},{8,43},{12,47},{16,51},{20,55},{24,59},{28,63},{1,32... | collective-permute-start | bytes 983048 | tf_op jit(solution)/shard_map/ppermute | solution.py:381
  74.3 1.7 %copy.14.weight = bf16[5120,64]{1,0:T(8,128)(2,1)S(1)} copy(bf16[5120,64]{0,1:T(8,128)(2,1)} %param.25) | data formatting | bytes 1310720 | tf_op args[12]
  75.9 1.7 %collective-permute-done.9.p1 = bf16[32,5120]{1,0:T(8,128)(2,1)} collective-permute-done((bf16[32,5120]{1,0:T(8,128)(2,1)}, bf16[32,5120]{1,0:T(8,128)(2,1)}, u32[]{:S(2)}, u32[]{:S(2)}) %collective-permute-start.9) | collective-permute-done | bytes 327712 | tf_op jit(solution)/shard_map/ppermute | solution.py:379
  77.7 4.9 %collective-permute-done.11.p2 = bf16[32,5120]{1,0:T(8,128)(2,1)} collective-permute-done((bf16[32,5120]{1,0:T(8,128)(2,1)}, bf16[32,5120]{1,0:T(8,128)(2,1)}, u32[]{:S(2)}, u32[]{:S(2)}) %collective-permute-start.11) | collective-permute-done | bytes 327712 | tf_op jit(solution)/shard_map/ppermute | solution.py:381
  82.6 0.0 copy-done
  82.6 0.0 copy-done.1
  82.6 0.0 copy-done.2
  82.6 0.0 copy-done.3
  82.6 0.0 copy-done.4
  82.6 1.9 %head.1 = f32[32,64]{1,0:T(8,128)S(1)} custom-call(s32[4]{0:T(128)S(1)} %copy-done.2, f32[4]{0:T(128)S(1)} %copy-done.3, s32[32]{0:T(128)S(1)} %copy-done.4, bf16[32,5120]{1,0:T(8,128)(2,1)S(1)} %get-tuple-element.15.p0, bf16[32,5120]{1,0:T(8,128)(2,1)} %collective-permute-done.9.p1, bf16[32,5120]{1,0:T(8,128)(2,1)} %collective-permute-done.11.p2, ...), custom_call_target="tpu_custom_call" | custom-call | tf_op jit(solution)/shard_map/head/pallas_call | solution.py:337
  84.5 1.3 %collective-permute-start.12 = (f32[32,64]{1,0:T(8,128)S(1)}, f32[32,64]{1,0:T(8,128)S(1)}, u32[]{:S(2)}, u32[]{:S(2)}) collective-permute-start(f32[32,64]{1,0:T(8,128)S(1)} %head.1), channel_id=1, source_target_pairs={{0,128},{64,192},{128,0},{192,64},{1,129},{65,193},{129,1},{193,65... | collective-permute-start | bytes 24584 | tf_op jit(solution)/shard_map/ppermute | solution.py:385
  85.9 2.2 %collective-permute-start.13 = (f32[32,64]{1,0:T(8,128)S(1)}, f32[32,64]{1,0:T(8,128)S(1)}, u32[]{:S(2)}, u32[]{:S(2)}) collective-permute-start(f32[32,64]{1,0:T(8,128)S(1)} %head.1), channel_id=1, source_target_pairs={{0,64},{64,128},{128,192},{192,0},{1,65},{65,129},{129,193},{193,1... | collective-permute-start | bytes 24584 | tf_op jit(solution)/shard_map/ppermute | solution.py:385
  88.0 0.0 collective-permute-start.14
  88.0 1.8 %collective-permute-done.12 = f32[32,64]{1,0:T(8,128)S(1)} collective-permute-done((f32[32,64]{1,0:T(8,128)S(1)}, f32[32,64]{1,0:T(8,128)S(1)}, u32[]{:S(2)}, u32[]{:S(2)}) %collective-permute-start.12) | collective-permute-done | bytes 8224 | tf_op jit(solution)/shard_map/ppermute | solution.py:385
  89.9 0.0 collective-permute-done.13
  89.9 3.1 %collective-permute-done.14 = f32[32,64]{1,0:T(8,128)S(1)} collective-permute-done((f32[32,64]{1,0:T(8,128)S(1)}, f32[32,64]{1,0:T(8,128)S(1)}, u32[]{:S(2)}, u32[]{:S(2)}) %collective-permute-start.14) | collective-permute-done | bytes 8224 | tf_op jit(solution)/shard_map/ppermute | solution.py:385
  93.0 0.6 add_add_fusion
  (2 shorter events, 0.0 us)
Async XLA Ops:
  0.0 1.7 %copy-start.5 = (bf16[1,128,640]{2,1,0:T(8,128)(2,1)S(1)}, bf16[1,128,640]{2,1,0:T(8,128)(2,1)}, u32[]{:S(2)}) copy-start(bf16[1,128,640]{2,1,0:T(8,128)(2,1)} %param.13) | copy-start | bytes 491524
  1.6 12.0 %collective-permute-start.1 = (bf16[1280,640]{1,0:T(8,128)(2,1)S(1)}, bf16[1280,640]{1,0:T(8,128)(2,1)S(1)}, u32[]{:S(2)}, u32[]{:S(2)}) collective-permute-start(bf16[1280,640]{1,0:T(8,128)(2,1)S(1)} %get-tuple-element.13.mine_pack), channel_id=1, source_target_pairs={{0,4},{4,0},{8,12},{12,8},{16,20},{20,16},{24,28},{28,24},{32,36},... | collective-permute-start | bytes 4915208 | tf_op jit(solution)/shard_map/ppermute | solution.py:366
  1.7 6.8 %collective-permute-start = (bf16[128,640]{1,0:T(8,128)(2,1)S(1)}, bf16[128,640]{1,0:T(8,128)(2,1)S(1)}, u32[]{:S(2)}, u32[]{:S(2)}) collective-permute-start(bf16[128,640]{1,0:T(8,128)(2,1)S(1)} %bitcast.14), channel_id=1, source_target_pairs={{0,32},{4,36},{8,40},{12,44},{16,48},{20,52},{24,56},{28,60},{32,0... | collective-permute-start | bytes 491528 | tf_op jit(solution)/shard_map/ppermute | solution.py:364
  8.5 10.9 %collective-permute-start.2 = (bf16[256,640]{1,0:T(8,128)(2,1)S(1)}, bf16[256,640]{1,0:T(8,128)(2,1)S(1)}, u32[]{:S(2)}, u32[]{:S(2)}) collective-permute-start(bf16[256,640]{1,0:T(8,128)(2,1)S(1)} %join.1.queries), channel_id=1, source_target_pairs={{0,8},{4,12},{8,16},{12,20},{16,24},{20,28},{24,0},{28,4},{32,40},... | collective-permute-start | bytes 983048 | tf_op jit(solution)/shard_map/ppermute | solution.py:369
  10.1 15.5 %collective-permute-start.4 = (bf16[256,640]{1,0:T(8,128)(2,1)S(1)}, bf16[256,640]{1,0:T(8,128)(2,1)S(1)}, u32[]{:S(2)}, u32[]{:S(2)}) collective-permute-start(bf16[256,640]{1,0:T(8,128)(2,1)S(1)} %join.1.queries), channel_id=1, source_target_pairs={{0,24},{4,28},{8,0},{12,4},{16,8},{20,12},{24,16},{28,20},{32,56},... | collective-permute-start | bytes 983048 | tf_op jit(solution)/shard_map/ppermute | solution.py:369
  11.8 17.1 %collective-permute-start.6 = (bf16[256,640]{1,0:T(8,128)(2,1)S(1)}, bf16[256,640]{1,0:T(8,128)(2,1)S(1)}, u32[]{:S(2)}, u32[]{:S(2)}) collective-permute-start(bf16[256,640]{1,0:T(8,128)(2,1)S(1)} %join.1.queries), channel_id=1, source_target_pairs={{0,16},{4,20},{8,24},{12,28},{16,0},{20,4},{24,8},{28,12},{32,48},... | collective-permute-start | bytes 983048 | tf_op jit(solution)/shard_map/ppermute | solution.py:369
  19.4 35.2 %slice-start = ((s8[6553600]{0:T(1024)(128)(4,1)}), s8[4194304]{0:T(1024)(128)(4,1)S(1)}, s32[]{:S(2)}) async-start(s8[6553600]{0:T(1024)(128)(4,1)} %bitcast.6), calls=%async_computation | async-start | bytes 8388608
  22.8 31.8 %slice-start.1 = ((s8[6553600]{0:T(1024)(128)(4,1)}), s8[2359296]{0:T(1024)(128)(4,1)S(1)}, s32[]{:S(2)}) async-start(s8[6553600]{0:T(1024)(128)(4,1)} %bitcast.6), calls=%async_computation.1 | async-start | bytes 4718592
  32.6 12.3 %collective-permute-start.7 = (bf16[1312,128]{1,0:T(8,128)(2,1)S(1)}, bf16[1312,128]{1,0:T(8,128)(2,1)S(1)}, u32[]{:S(2)}, u32[]{:S(2)}) collective-permute-start(bf16[1312,128]{1,0:T(8,128)(2,1)S(1)} %attend.7), channel_id=1, source_target_pairs={{0,16},{4,20},{8,24},{12,28},{16,0},{20,4},{24,8},{28,12},{32,48},... | collective-permute-start | bytes 1007624 | tf_op jit(solution)/shard_map/ppermute | solution.py:375
  32.7 15.6 %collective-permute-start.5 = (bf16[1312,128]{1,0:T(8,128)(2,1)S(1)}, bf16[1312,128]{1,0:T(8,128)(2,1)S(1)}, u32[]{:S(2)}, u32[]{:S(2)}) collective-permute-start(bf16[1312,128]{1,0:T(8,128)(2,1)S(1)} %attend.6.rest_0_), channel_id=1, source_target_pairs={{0,8},{4,12},{8,16},{12,20},{16,24},{20,28},{24,0},{28,4},{32,40},... | collective-permute-start | bytes 1007624 | tf_op jit(solution)/shard_map/ppermute | solution.py:375
  37.2 11.2 %collective-permute-start.3 = (bf16[1312,128]{1,0:T(8,128)(2,1)S(1)}, bf16[1312,128]{1,0:T(8,128)(2,1)S(1)}, u32[]{:S(2)}, u32[]{:S(2)}) collective-permute-start(bf16[1312,128]{1,0:T(8,128)(2,1)S(1)} %attend.5.rest_0_), channel_id=1, source_target_pairs={{0,24},{4,28},{8,0},{12,4},{16,8},{20,12},{24,16},{28,20},{32,56},... | collective-permute-start | bytes 1007624 | tf_op jit(solution)/shard_map/ppermute | solution.py:375
  48.5 6.1 %collective-permute-start.8 = (bf16[656,128]{1,0:T(8,128)(2,1)S(1)}, bf16[656,128]{1,0:T(8,128)(2,1)S(1)}, u32[]{:S(2)}, u32[]{:S(2)}) collective-permute-start(bf16[656,128]{1,0:T(8,128)(2,1)S(1)} %merge.1), channel_id=1, source_target_pairs={{0,32},{4,36},{8,40},{12,44},{16,48},{20,52},{24,56},{28,60},{32,0... | collective-permute-start | bytes 503816 | tf_op jit(solution)/shard_map/ppermute | solution.py:376
  56.7 25.9 %copy-start = (f32[32,2,5120]{2,1,0:T(2,128)S(1)}, f32[32,2,5120]{2,1,0:T(2,128)}, u32[]{:S(2)}) copy-start(f32[32,2,5120]{2,1,0:T(2,128)} %table.1) | copy-start | bytes 3932164
  56.7 25.9 %copy-start.1 = (bf16[1,32,5120]{2,1,0:T(8,128)(2,1)S(1)}, bf16[1,32,5120]{2,1,0:T(8,128)(2,1)}, u32[]{:S(2)}) copy-start(bf16[1,32,5120]{2,1,0:T(8,128)(2,1)} %param.22) | copy-start | bytes 983044
  56.7 25.9 %copy-start.2 = (s32[4]{0:T(128)S(1)}, s32[4]{0:T(128)}, u32[]{:S(2)}) copy-start(s32[4]{0:T(128)} %group_branch.3) | copy-start | bytes 52
  56.7 25.9 %copy-start.3 = (f32[4]{0:T(128)S(1)}, f32[4]{0:T(128)}, u32[]{:S(2)}) copy-start(f32[4]{0:T(128)} %guidance_w.1) | copy-start | bytes 52
  56.8 25.9 %copy-start.4 = (s32[32]{0:T(128)S(1)}, s32[32]{0:T(128)}, u32[]{:S(2)}) copy-start(s32[32]{0:T(128)} %frame_level.1) | copy-start | bytes 388
  56.8 13.8 %collective-permute-start.10 = (bf16[32,5120]{1,0:T(8,128)(2,1)S(1)}, bf16[32,5120]{1,0:T(8,128)(2,1)S(1)}, u32[]{:S(2)}, u32[]{:S(2)}) collective-permute-start(bf16[32,5120]{1,0:T(8,128)(2,1)S(1)} %get-tuple-element.18), channel_id=1, source_target_pairs={{0,3},{4,7},{8,11},{12,15},{16,19},{20,23},{24,27},{28,31},{1,0},{... | collective-permute-start | bytes 983048 | tf_op jit(solution)/shard_map/ppermute | solution.py:378
  62.4 15.3 %collective-permute-start.9 = (bf16[32,5120]{1,0:T(8,128)(2,1)}, bf16[32,5120]{1,0:T(8,128)(2,1)}, u32[]{:S(2)}, u32[]{:S(2)}) collective-permute-start(bf16[32,5120]{1,0:T(8,128)(2,1)} %get-tuple-element.16), channel_id=1, source_target_pairs={{0,3},{4,7},{8,11},{12,15},{16,19},{20,23},{24,27},{28,31},{1,0},{... | collective-permute-start | bytes 983048 | tf_op jit(solution)/shard_map/ppermute | solution.py:379
  71.3 11.2 %collective-permute-start.11 = (bf16[32,5120]{1,0:T(8,128)(2,1)}, bf16[32,5120]{1,0:T(8,128)(2,1)}, u32[]{:S(2)}, u32[]{:S(2)}) collective-permute-start(bf16[32,5120]{1,0:T(8,128)(2,1)} %add_convert_fusion), channel_id=1, source_target_pairs={{0,35},{4,39},{8,43},{12,47},{16,51},{20,55},{24,59},{28,63},{1,32... | collective-permute-start | bytes 983048 | tf_op jit(solution)/shard_map/ppermute | solution.py:381
  84.5 5.3 %collective-permute-start.12 = (f32[32,64]{1,0:T(8,128)S(1)}, f32[32,64]{1,0:T(8,128)S(1)}, u32[]{:S(2)}, u32[]{:S(2)}) collective-permute-start(f32[32,64]{1,0:T(8,128)S(1)} %head.1), channel_id=1, source_target_pairs={{0,128},{64,192},{128,0},{192,64},{1,129},{65,193},{129,1},{193,65... | collective-permute-start | bytes 24584 | tf_op jit(solution)/shard_map/ppermute | solution.py:385
  85.9 4.0 %collective-permute-start.13 = (f32[32,64]{1,0:T(8,128)S(1)}, f32[32,64]{1,0:T(8,128)S(1)}, u32[]{:S(2)}, u32[]{:S(2)}) collective-permute-start(f32[32,64]{1,0:T(8,128)S(1)} %head.1), channel_id=1, source_target_pairs={{0,64},{64,128},{128,192},{192,0},{1,65},{65,129},{129,193},{193,1... | collective-permute-start | bytes 24584 | tf_op jit(solution)/shard_map/ppermute | solution.py:385
  88.0 4.9 %collective-permute-start.14 = (f32[32,64]{1,0:T(8,128)S(1)}, f32[32,64]{1,0:T(8,128)S(1)}, u32[]{:S(2)}, u32[]{:S(2)}) collective-permute-start(f32[32,64]{1,0:T(8,128)S(1)} %head.1), channel_id=1, source_target_pairs={{0,192},{64,0},{128,64},{192,128},{1,193},{65,1},{129,65},{193,129... | collective-permute-start | bytes 24584 | tf_op jit(solution)/shard_map/ppermute | solution.py:385

commit v3 on v2

--- a/solution.py
+++ b/solution.py
@@ -51,29 +51,20 @@
     return [(i, (i + step) % count) for i in range(count)]
 
 
-def join_kernel(here, there, out):
-    step = here.shape[0] // MPS
-    mine = lax.axis_index("mp")
-    side = lax.axis_index("seq") // (XS * 2)
-    at = 0
-    for first, second, toward in ((there, here, 3 - 2 * side), (here, there, 1 + 2 * side)):
-        for ref, k in ((first, toward), (first, 2), (second, toward), (second, 0)):
-            start = pl.multiple_of(lax.rem(mine + k, MPS) * step, step)
-            out[at : at + step, :] = ref[pl.ds(start, step), :]
-            at += step
-
-
-def join(here, there):
-    rows, feat = here.shape
-    vmem = pl.BlockSpec(memory_space=pltpu.VMEM)
-    return pl.pallas_call(
-        join_kernel,
-        out_shape=jax.ShapeDtypeStruct((2 * rows, feat), here.dtype),
-        in_specs=[vmem] * 2,
+def hold_kernel(source, *rest):
+    rest[-1][...] = source[...]
+
+
+def hold(source, after):
+    vmem = pl.BlockSpec(memory_space=pltpu.VMEM)
+    return pl.pallas_call(
+        hold_kernel,
+        out_shape=jax.ShapeDtypeStruct(source.shape, source.dtype),
+        in_specs=[vmem] + [pl.BlockSpec(memory_space=pl.ANY)] * len(after),
         out_specs=vmem,
         compiler_params=pltpu.CompilerParams(vmem_limit_bytes=4 * 2**20),
-        name="join",
-    )(here, there)
+        name="hold",
+    )(source, *after)
 
 
 def pack_kernel(
@@ -86,9 +77,10 @@
     group_branch,
     out,
     bias,
-    held,
+    queries,
     near_v,
     far_v,
+    held,
     lens,
     order,
     sems,
@@ -118,6 +110,12 @@
     out[count:, near:] = far_v[...].T
     for fetch in fetches[2:]:
         fetch.wait()
+    step = held.shape[0] // MPS
+    mine = lax.axis_index("mp")
+    side = lax.axis_index("seq") // (XS * 2)
+    for i, k in enumerate((3 - 2 * side, 0, 1 + 2 * side, 2)):
+        start = pl.multiple_of(lax.rem(mine + k, MPS) * step, step)
+        queries[i * step : (i + 1) * step, :] = held[pl.ds(start, step), :]
     length = lens[order[lax.axis_index("branch")]]
     seq = lax.axis_index("seq")
     lanes = bias.shape[1]
@@ -144,6 +142,7 @@
         scratch_shapes=[
             pltpu.VMEM((near, feat), span_v.dtype),
             pltpu.VMEM((far, feat), hist_v.dtype),
+            pltpu.VMEM(span_q.shape, span_q.dtype),
             pltpu.SMEM(hist_len.shape, jnp.int32),
             pltpu.SMEM(group_branch.shape, jnp.int32),
             pltpu.SemaphoreType.DMA((7,)),
@@ -159,17 +158,20 @@
     )
 
 
-def attend_kernel(queries, mine_pack, core_pack, bias, *rest):
+def attend_kernel(here, there, mine_pack, core_pack, bias, *rest):
     sent = rest[-1]
     packs = (mine_pack, core_pack)
-    feat = queries.shape[1]
-    rows = queries.shape[0] // 2
+    rows, feat = here.shape
+    half = rows // 2
     heads = feat // HSZ
     count = mine_pack.shape[0] - feat
     levels = []
-    for h in range(heads):
+
+    def scores_of(h):
         cols = slice(h * HSZ, (h + 1) * HSZ)
-        q = queries[:, cols]
+        q = jnp.concatenate(
+            [there[half:, cols], here[:half, cols], here[half:, cols], there[:half, cols]], axis=0
+        )
         scores = []
         for i, pack_ref in enumerate(packs):
             s = lax.dot_general(
@@ -180,6 +182,13 @@
             )
             offset = bias[i * count : (i + 1) * count, :]
             scores.append(s + jnp.concatenate([offset] * (s.shape[1] // LANES), axis=1))
+        return scores
+
+    coming = scores_of(0)
+    for h in range(heads):
+        scores = coming
+        if h + 1 < heads:
+            coming = scores_of(h + 1)
         peak = functools.reduce(jnp.maximum, [jnp.max(s, axis=0, keepdims=True) for s in scores])
         total, summed = 0.0, 0.0
         for pack_ref, s in zip(packs, scores):
@@ -210,13 +219,13 @@
 
 
 def attend(queries, packs, bias, after):
-    rows, feat = queries.shape[0] // 2, queries.shape[1]
+    rows, feat = queries[0].shape
     count = packs[0].shape[0] - feat
     vmem = pl.BlockSpec(memory_space=pltpu.VMEM)
     return pl.pallas_call(
         attend_kernel,
         out_shape=jax.ShapeDtypeStruct((2 * (feat + STAT_ROWS), rows), jnp.bfloat16),
-        in_specs=[vmem] * 4 + [pl.BlockSpec(memory_space=pl.ANY)] * len(after),
+        in_specs=[vmem] * 5 + [pl.BlockSpec(memory_space=pl.ANY)] * len(after),
         out_specs=vmem,
         compiler_params=pltpu.CompilerParams(vmem_limit_bytes=16 * 2**20),
         cost_estimate=pl.CostEstimate(
@@ -225,7 +234,7 @@
             transcendentals=4 * rows * count * (feat // HSZ),
         ),
         name="attend",
-    )(queries, *packs, bias, *after)
+    )(*queries, *packs, bias, *after)
 
 
 def merged(parts, heads):
@@ -360,17 +369,25 @@
     mod_table,
     head_weight,
 ):
-    mine = span_q[0]
+    own, bias, mine = pack(
+        span_q[0], span_k[0], span_v[0], hist_k[0], hist_v[0], hist_len, group_branch
+    )
+    packs = [own, lax.ppermute(own, "seq", hop(0, 0, 1))]
     across = lax.ppermute(mine, "seq", hop(1, 0, 0))
-    own, bias, held = pack(mine, span_k[0], span_v[0], hist_k[0], hist_v[0], hist_len, group_branch)
-    packs = [own, lax.ppermute(own, "seq", hop(0, 0, 1))]
-    pairs = {0: join(held, across)}
-    for dx in (1, 3, 2):
-        pairs[dx] = lax.ppermute(pairs[0], "seq", hop(0, dx, 0))
+    up, down = hop(0, 1, 0), hop(0, 3, 0)
+    mine_up, mine_down = lax.ppermute(mine, "seq", up), lax.ppermute(mine, "seq", down)
+    ready = hold(across, [mine_up, mine_down])
+    across_up, across_down = lax.ppermute(ready, "seq", up), lax.ppermute(ready, "seq", down)
+    pairs = {
+        0: (mine, across),
+        1: (mine_up, across_up),
+        3: (mine_down, across_down),
+        2: (lax.ppermute(mine_up, "seq", up), lax.ppermute(across_down, "seq", down)),
+    }
     parts = []
     made = []
     for dx in (0, 1, 3, 2):
-        sent = attend(pairs[dx], packs, bias, made[-1:])
+        sent = attend(pairs[dx], packs, bias, ())
         made.append(sent)
         parts.append(lax.ppermute(sent, "seq", hop(0, -dx, 0)) if dx else sent)
     parts.append(lax.ppermute(merge(parts), "seq", hop(1, 0, 0)))

time: 93.7 us -> 85.4 us (0.911)
  waiting for transfers between devices: 44 us -> 34.9 us
  starting transfers between devices: 26.8 us -> 31.1 us
  Pallas kernels: 19.5 us -> 16 us
    ppermute x3, waiting for transfers between devices: 11.2 us -> 3.98 us  [body(): parts.append(lax.ppermute(sent, 'seq', hop(0, -dx, 0)) if dx else sent)]
    ppermute x3 -> x6, starting transfers between devices: 5.13 us -> 10 us  [the longest x1 3.69 us: body(): lax.ppermute(across_down, 'seq', down)]
    ppermute x3 -> x6, waiting for transfers between devices: 5.11 us -> 9.73 us  [the longest x1 2.83 us: body(): lax.ppermute(ready, 'seq', down)]
    ppermute x1, waiting for transfers between devices: 4.76 us -> 0.17 us  [body(): across = lax.ppermute(mine, 'seq', hop(1, 0, 0))]
    pallas_call x4, Pallas kernels: 13.7 us -> 10.3 us  [attend(): pl.pallas_call(attend_kernel, out_shape=jax.ShapeDtypeStruct((2 * (feat +...]
    ppermute x1, waiting for transfers between devices: 1.73 us -> 0.01 us  [body(): aside = lax.ppermute(side_block, ('seq', 'mp'), pair_hop(onward))]
    ppermute x1, starting transfers between devices: 1.49 us -> 0.39 us  [body(): parts.append(lax.ppermute(merge(parts), 'seq', hop(1, 0, 0)))]
    ppermute x3, starting transfers between devices: 4.61 us -> 5.57 us  [body(): parts.append(lax.ppermute(sent, 'seq', hop(0, -dx, 0)) if dx else sent)]
  transfers between devices with their start and end apart: 15 -> 18, of which waited for: 11 -> 12; matrix products, arithmetic and copies ran while one was open for 3% -> 3% of each run, Pallas kernels for 11% -> 12%
where the time goes in v3:
time: 85.4 us; the launch traced here: 85.3 us
  waiting for transfers between devices  34.9 us (41%)
  starting transfers between devices  31.1 us (36%)
  Pallas kernels  16 us (19%)
  local copies, waits for them, and re-layouts  1.68 us (2%)
  other arithmetic  1.42 us (2%)
    pallas_call x4, Pallas kernels, attend(): pl.pallas_call(attend_kernel, out_shape=jax.ShapeDtypeStruct((2 * (feat +...  10.3 us
    ppermute x1, waiting for transfers between devices, body(): passed = lax.ppermute(far_block, ('seq', 'mp'), pair_hop(onward))  6.72 us
    ppermute x3, starting transfers between devices, body(): parts.append(lax.ppermute(sent, 'seq', hop(0, -dx, 0)) if dx else sent)  5.57 us
    ppermute x1, starting transfers between devices, body(): passed = lax.ppermute(far_block, ('seq', 'mp'), pair_hop(onward))  5.48 us
    ppermute x1, waiting for transfers between devices, body(): parts.append(lax.ppermute(merge(parts), 'seq', hop(1, 0, 0)))  5.06 us
    ppermute x3, waiting for transfers between devices, body(): around = [lax.ppermute(velocity, 'branch', turn(k)) for k in (1, 3, 2)]  4.95 us
    ppermute x1, waiting for transfers between devices, body(): lax.ppermute(joined, ('seq', 'mp'), pair_hop(across_onward))  4.25 us
    ppermute x3, waiting for transfers between devices, body(): parts.append(lax.ppermute(sent, 'seq', hop(0, -dx, 0)) if dx else sent)  3.98 us
  transfers between devices with their start and end apart: 18, of which 12 were waited for; matrix products, arithmetic and copies ran while one was open for 3% of the time, Pallas kernels for 12%

profile of v3, /device:TPU:24, one launch (start us, length us, event | category | flops | bytes accessed | tf_op | source)
XLA Modules:
  0.0 85.3 jit_solution(3361450086835672593)
XLA Ops:
  0.0 1.6 %pack.1 = (bf16[1280,640]{1,0:T(8,128)(2,1)S(1)}, f32[1280,128]{1,0:T(8,128)S(1)}, bf16[128,640]{1,0:T(8,128)(2,1)S(1)}) custom-call(bf16[128,640]{1,0:T(8,128)(2,1)} %bitcast.11, bf16[128,640]{1,0:T(8,128)(2,1)} %bitcast.12, bf16[128,640]{1,0:T(8,128)(2,1)} %bitcast.13, bf16[512,640]{1,0:T(8,128)(2,1)} %bitcast.9, bf16[512,640]{1,0:T(8,128)(2,1)} %bitcast.10, ...), custom_call_target="tpu_custom_call" | custom-call | flops 6000000000 | bytes 1638400 | tf_op jit(solution)/shard_map/pack/pallas_call | solution.py:133
  1.6 0.1 collective-permute-start.1
  1.7 1.6 %collective-permute-start.2 = (bf16[128,640]{1,0:T(8,128)(2,1)S(1)}, bf16[128,640]{1,0:T(8,128)(2,1)S(1)}, u32[]{:S(2)}, u32[]{:S(2)}) collective-permute-start(bf16[128,640]{1,0:T(8,128)(2,1)S(1)} %get-tuple-element.12.here), channel_id=1, source_target_pairs={{0,8},{4,12},{8,16},{12,20},{16,24},{20,28},{24,0},{28,4},{32,40},... | collective-permute-start | bytes 491528 | tf_op jit(solution)/shard_map/ppermute | solution.py:378
  3.3 1.9 %collective-permute-start = (bf16[128,640]{1,0:T(8,128)(2,1)S(1)}, bf16[128,640]{1,0:T(8,128)(2,1)S(1)}, u32[]{:S(2)}, u32[]{:S(2)}) collective-permute-start(bf16[128,640]{1,0:T(8,128)(2,1)S(1)} %get-tuple-element.12.here), channel_id=1, source_target_pairs={{0,32},{4,36},{8,40},{12,44},{16,48},{20,52},{24,56},{28,60},{32,0... | collective-permute-start | bytes 491528 | tf_op jit(solution)/shard_map/ppermute | solution.py:376
  5.2 1.7 %collective-permute-start.3 = (bf16[128,640]{1,0:T(8,128)(2,1)S(1)}, bf16[128,640]{1,0:T(8,128)(2,1)S(1)}, u32[]{:S(2)}, u32[]{:S(2)}) collective-permute-start(bf16[128,640]{1,0:T(8,128)(2,1)S(1)} %get-tuple-element.12.here), channel_id=1, source_target_pairs={{0,24},{4,28},{8,0},{12,4},{16,8},{20,12},{24,16},{28,20},{32,56},... | collective-permute-start | bytes 491528 | tf_op jit(solution)/shard_map/ppermute | solution.py:378
  6.9 2.6 %collective-permute-done.2.rest_0_.here = bf16[128,640]{1,0:T(8,128)(2,1)S(1)} collective-permute-done((bf16[128,640]{1,0:T(8,128)(2,1)S(1)}, bf16[128,640]{1,0:T(8,128)(2,1)S(1)}, u32[]{:S(2)}, u32[]{:S(2)}) %collective-permute-start.2) | collective-permute-done | bytes 163872 | tf_op jit(solution)/shard_map/ppermute | solution.py:378
  9.5 0.2 collective-permute-done.there.source
  9.7 1.5 %collective-permute-done.3.rest_1_.here = bf16[128,640]{1,0:T(8,128)(2,1)S(1)} collective-permute-done((bf16[128,640]{1,0:T(8,128)(2,1)S(1)}, bf16[128,640]{1,0:T(8,128)(2,1)S(1)}, u32[]{:S(2)}, u32[]{:S(2)}) %collective-permute-start.3) | collective-permute-done | bytes 163872 | tf_op jit(solution)/shard_map/ppermute | solution.py:378
  11.2 3.0 %collective-permute-start.6 = (bf16[128,640]{1,0:T(8,128)(2,1)S(1)}, bf16[128,640]{1,0:T(8,128)(2,1)S(1)}, u32[]{:S(2)}, u32[]{:S(2)}) collective-permute-start(bf16[128,640]{1,0:T(8,128)(2,1)S(1)} %hold.1), channel_id=1, source_target_pairs={{0,24},{4,28},{8,0},{12,4},{16,8},{20,12},{24,16},{28,20},{32,56},... | collective-permute-start | bytes 491528 | tf_op jit(solution)/shard_map/ppermute | solution.py:380
  14.2 0.0 collective-permute-start.8
  14.2 2.8 %collective-permute-done.6.there = bf16[128,640]{1,0:T(8,128)(2,1)S(1)} collective-permute-done((bf16[128,640]{1,0:T(8,128)(2,1)S(1)}, bf16[128,640]{1,0:T(8,128)(2,1)S(1)}, u32[]{:S(2)}, u32[]{:S(2)}) %collective-permute-start.6) | collective-permute-done | bytes 163872 | tf_op jit(solution)/shard_map/ppermute | solution.py:380
  17.1 3.7 %collective-permute-start.9 = (bf16[128,640]{1,0:T(8,128)(2,1)S(1)}, bf16[128,640]{1,0:T(8,128)(2,1)S(1)}, u32[]{:S(2)}, u32[]{:S(2)}) collective-permute-start(bf16[128,640]{1,0:T(8,128)(2,1)S(1)} %collective-permute-done.6.there), channel_id=1, source_target_pairs={{0,24},{4,28},{8,0},{12,4},{16,8},{20,12},{24,16},{28,20},{32,56},... | collective-permute-start | bytes 491528 | tf_op jit(solution)/shard_map/ppermute | solution.py:385
  20.7 0.0 collective-permute-start.4
  20.7 0.0 collective-permute-done.8.here
  20.7 2.8 %collective-permute-done.9.there = bf16[128,640]{1,0:T(8,128)(2,1)S(1)} collective-permute-done((bf16[128,640]{1,0:T(8,128)(2,1)S(1)}, bf16[128,640]{1,0:T(8,128)(2,1)S(1)}, u32[]{:S(2)}, u32[]{:S(2)}) %collective-permute-start.9) | collective-permute-done | bytes 163872 | tf_op jit(solution)/shard_map/ppermute | solution.py:385
  23.6 0.0 collective-permute-done.1.core_pack
  23.6 2.6 %attend.7 = bf16[1312,128]{1,0:T(8,128)(2,1)S(1)} custom-call(bf16[128,640]{1,0:T(8,128)(2,1)S(1)} %collective-permute-done.8.here, bf16[128,640]{1,0:T(8,128)(2,1)S(1)} %collective-permute-done.9.there, bf16[1280,640]{1,0:T(8,128)(2,1)S(1)} %get-tuple-element.13.mine_pack, bf16[1280,640]{1,0:T(8,128)(2,1)S(1)} %collective-permute-done.1.core_pack, ...), custom_call_target="tpu_custom_call" | custom-call | flops 838860800 | bytes 3276800 | tf_op jit(solution)/shard_map/attend/pallas_call | solution.py:225
  26.2 2.0 %collective-permute-start.10 = (bf16[1312,128]{1,0:T(8,128)(2,1)S(1)}, bf16[1312,128]{1,0:T(8,128)(2,1)S(1)}, u32[]{:S(2)}, u32[]{:S(2)}) collective-permute-start(bf16[1312,128]{1,0:T(8,128)(2,1)S(1)} %attend.7), channel_id=1, source_target_pairs={{0,16},{4,20},{8,24},{12,28},{16,0},{20,4},{24,8},{28,12},{32,48},... | collective-permute-start | bytes 1007624 | tf_op jit(solution)/shard_map/ppermute | solution.py:392
  28.2 0.0 slice-start
  28.2 2.6 %attend.6 = bf16[1312,128]{1,0:T(8,128)(2,1)S(1)} custom-call(bf16[128,640]{1,0:T(8,128)(2,1)S(1)} %collective-permute-done.3.rest_1_.here, bf16[128,640]{1,0:T(8,128)(2,1)S(1)} %collective-permute-done.6.there, bf16[1280,640]{1,0:T(8,128)(2,1)S(1)} %get-tuple-element.13.mine_pack, bf16[1280,640]{1,0:T(8,128)(2,1)S(1)} %collective-permute-done.1.core_pack, ...), custom_call_target="tpu_custom_call" | custom-call | flops 838860800 | bytes 3276800 | tf_op jit(solution)/shard_map/attend/pallas_call | solution.py:225
  30.7 0.0 slice-start.1
  30.8 2.9 %collective-permute-start.7 = (bf16[1312,128]{1,0:T(8,128)(2,1)S(1)}, bf16[1312,128]{1,0:T(8,128)(2,1)S(1)}, u32[]{:S(2)}, u32[]{:S(2)}) collective-permute-start(bf16[1312,128]{1,0:T(8,128)(2,1)S(1)} %attend.6), channel_id=1, source_target_pairs={{0,8},{4,12},{8,16},{12,20},{16,24},{20,28},{24,0},{28,4},{32,40},... | collective-permute-start | bytes 1007624 | tf_op jit(solution)/shard_map/ppermute | solution.py:392
  33.6 0.0 collective-permute-done.4.there
  33.6 2.6 %attend.5 = bf16[1312,128]{1,0:T(8,128)(2,1)S(1)} custom-call(bf16[128,640]{1,0:T(8,128)(2,1)S(1)} %collective-permute-done.2.rest_0_.here, bf16[128,640]{1,0:T(8,128)(2,1)S(1)} %collective-permute-done.4.there, bf16[1280,640]{1,0:T(8,128)(2,1)S(1)} %get-tuple-element.13.mine_pack, bf16[1280,640]{1,0:T(8,128)(2,1)S(1)} %collective-permute-done.1.core_pack, ...), custom_call_target="tpu_custom_call" | custom-call | flops 838860800 | bytes 3276800 | tf_op jit(solution)/shard_map/attend/pallas_call | solution.py:225
  36.2 0.7 collective-permute-start.5
  36.9 2.6 %attend.4.refs_0_ = bf16[1312,128]{1,0:T(8,128)(2,1)S(1)} custom-call(bf16[128,640]{1,0:T(8,128)(2,1)S(1)} %get-tuple-element.12.here, bf16[128,640]{1,0:T(8,128)(2,1)S(1)} %collective-permute-done.there.source, bf16[1280,640]{1,0:T(8,128)(2,1)S(1)} %get-tuple-element.13.mine_pack, bf16[1280,640]{1,0:T(8,128)(2,1)S(1)} %collective-permute-done.1.core_pack, ...), custom_call_target="tpu_custom_call" | custom-call | flops 838860800 | bytes 3276800 | tf_op jit(solution)/shard_map/attend/pallas_call | solution.py:225
  39.5 0.0 collective-permute-done.10.refs_3_
  39.5 2.6 %collective-permute-done.7.refs_2_ = bf16[1312,128]{1,0:T(8,128)(2,1)S(1)} collective-permute-done((bf16[1312,128]{1,0:T(8,128)(2,1)S(1)}, bf16[1312,128]{1,0:T(8,128)(2,1)S(1)}, u32[]{:S(2)}, u32[]{:S(2)}) %collective-permute-start.7) | collective-permute-done | bytes 335904 | tf_op jit(solution)/shard_map/ppermute | solution.py:392
  42.1 1.3 %collective-permute-done.5.refs_1_ = bf16[1312,128]{1,0:T(8,128)(2,1)S(1)} collective-permute-done((bf16[1312,128]{1,0:T(8,128)(2,1)S(1)}, bf16[1312,128]{1,0:T(8,128)(2,1)S(1)}, u32[]{:S(2)}, u32[]{:S(2)}) %collective-permute-start.5) | collective-permute-done | bytes 335904 | tf_op jit(solution)/shard_map/ppermute | solution.py:392
  43.5 0.2 merge.1
  43.6 0.4 collective-permute-start.11
  44.0 5.1 %collective-permute-done.11.refs_4_ = bf16[656,128]{1,0:T(8,128)(2,1)S(1)} collective-permute-done((bf16[656,128]{1,0:T(8,128)(2,1)S(1)}, bf16[656,128]{1,0:T(8,128)(2,1)S(1)}, u32[]{:S(2)}, u32[]{:S(2)}) %collective-permute-start.11) | collective-permute-done | bytes 167968 | tf_op jit(solution)/shard_map/ppermute | solution.py:393
  49.1 0.0 slice-done
  49.1 0.0 slice-done.1
  49.1 2.1 %project.1 = (bf16[32,5120]{1,0:T(8,128)(2,1)S(1)}, bf16[32,5120]{1,0:T(8,128)(2,1)S(1)}, bf16[32,5120]{1,0:T(8,128)(2,1)}, bf16[32,5120]{1,0:T(8,128)(2,1)S(1)}) custom-call(bf16[1312,128]{1,0:T(8,128)(2,1)S(1)} %attend.4.refs_0_, bf16[1312,128]{1,0:T(8,128)(2,1)S(1)} %collective-permute-done.5.refs_1_, ...), custom_call_target="tpu_custom_call" | custom-call | flops 838860800 | bytes 6553600 | tf_op jit(solution)/shard_map/project/pallas_call | solution.py:307
  51.2 0.0 copy-start
  51.2 0.0 copy-start.1
  51.2 0.0 copy-start.2
  51.2 0.0 copy-start.3
  51.2 0.0 copy-start.4
  51.2 5.5 %collective-permute-start.13 = (bf16[32,5120]{1,0:T(8,128)(2,1)S(1)}, bf16[32,5120]{1,0:T(8,128)(2,1)S(1)}, u32[]{:S(2)}, u32[]{:S(2)}) collective-permute-start(bf16[32,5120]{1,0:T(8,128)(2,1)S(1)} %get-tuple-element.18), channel_id=1, source_target_pairs={{0,3},{4,7},{8,11},{12,15},{16,19},{20,23},{24,27},{28,31},{1,0},{... | collective-permute-start | bytes 983048 | tf_op jit(solution)/shard_map/ppermute | solution.py:395
  56.7 1.4 %collective-permute-start.12 = (bf16[32,5120]{1,0:T(8,128)(2,1)}, bf16[32,5120]{1,0:T(8,128)(2,1)}, u32[]{:S(2)}, u32[]{:S(2)}) collective-permute-start(bf16[32,5120]{1,0:T(8,128)(2,1)} %get-tuple-element.16), channel_id=1, source_target_pairs={{0,3},{4,7},{8,11},{12,15},{16,19},{20,23},{24,27},{28,31},{1,0},{... | collective-permute-start | bytes 983048 | tf_op jit(solution)/shard_map/ppermute | solution.py:396
  58.1 6.7 %collective-permute-done.13 = bf16[32,5120]{1,0:T(8,128)(2,1)S(1)} collective-permute-done((bf16[32,5120]{1,0:T(8,128)(2,1)S(1)}, bf16[32,5120]{1,0:T(8,128)(2,1)S(1)}, u32[]{:S(2)}, u32[]{:S(2)}) %collective-permute-start.13) | collective-permute-done | bytes 327712 | tf_op jit(solution)/shard_map/ppermute | solution.py:395
  64.9 0.8 add_convert_fusion
  65.7 2.7 %collective-permute-start.14 = (bf16[32,5120]{1,0:T(8,128)(2,1)}, bf16[32,5120]{1,0:T(8,128)(2,1)}, u32[]{:S(2)}, u32[]{:S(2)}) collective-permute-start(bf16[32,5120]{1,0:T(8,128)(2,1)} %add_convert_fusion), channel_id=1, source_target_pairs={{0,35},{4,39},{8,43},{12,47},{16,51},{20,55},{24,59},{28,63},{1,32... | collective-permute-start | bytes 983048 | tf_op jit(solution)/shard_map/ppermute | solution.py:398
  68.3 1.7 %copy.14.weight = bf16[5120,64]{1,0:T(8,128)(2,1)S(1)} copy(bf16[5120,64]{0,1:T(8,128)(2,1)} %param.25) | data formatting | bytes 1310720 | tf_op args[12]
  70.0 0.0 collective-permute-done.12.p1
  70.0 4.3 %collective-permute-done.14.p2 = bf16[32,5120]{1,0:T(8,128)(2,1)} collective-permute-done((bf16[32,5120]{1,0:T(8,128)(2,1)}, bf16[32,5120]{1,0:T(8,128)(2,1)}, u32[]{:S(2)}, u32[]{:S(2)}) %collective-permute-start.14) | collective-permute-done | bytes 327712 | tf_op jit(solution)/shard_map/ppermute | solution.py:398
  74.3 0.0 copy-done
  74.3 0.0 copy-done.1
  74.3 0.0 copy-done.2
  74.3 0.0 copy-done.3
  74.3 0.0 copy-done.4
  74.3 1.9 %head.1 = f32[32,64]{1,0:T(8,128)S(1)} custom-call(s32[4]{0:T(128)S(1)} %copy-done.2, f32[4]{0:T(128)S(1)} %copy-done.3, s32[32]{0:T(128)S(1)} %copy-done.4, bf16[32,5120]{1,0:T(8,128)(2,1)S(1)} %get-tuple-element.15.p0, bf16[32,5120]{1,0:T(8,128)(2,1)} %collective-permute-done.12.p1, bf16[32,5120]{1,0:T(8,128)(2,1)} %collective-permute-done.14.p2, ...), custom_call_target="tpu_custom_call" | custom-call | tf_op jit(solution)/shard_map/head/pallas_call | solution.py:346
  76.2 1.3 %collective-permute-start.15 = (f32[32,64]{1,0:T(8,128)S(1)}, f32[32,64]{1,0:T(8,128)S(1)}, u32[]{:S(2)}, u32[]{:S(2)}) collective-permute-start(f32[32,64]{1,0:T(8,128)S(1)} %head.1), channel_id=1, source_target_pairs={{0,128},{64,192},{128,0},{192,64},{1,129},{65,193},{129,1},{193,65... | collective-permute-start | bytes 24584 | tf_op jit(solution)/shard_map/ppermute | solution.py:402
  77.5 2.2 %collective-permute-start.16 = (f32[32,64]{1,0:T(8,128)S(1)}, f32[32,64]{1,0:T(8,128)S(1)}, u32[]{:S(2)}, u32[]{:S(2)}) collective-permute-start(f32[32,64]{1,0:T(8,128)S(1)} %head.1), channel_id=1, source_target_pairs={{0,64},{64,128},{128,192},{192,0},{1,65},{65,129},{129,193},{193,1... | collective-permute-start | bytes 24584 | tf_op jit(solution)/shard_map/ppermute | solution.py:402
  79.7 0.0 collective-permute-start.17
  79.7 1.8 %collective-permute-done.15 = f32[32,64]{1,0:T(8,128)S(1)} collective-permute-done((f32[32,64]{1,0:T(8,128)S(1)}, f32[32,64]{1,0:T(8,128)S(1)}, u32[]{:S(2)}, u32[]{:S(2)}) %collective-permute-start.15) | collective-permute-done | bytes 8224 | tf_op jit(solution)/shard_map/ppermute | solution.py:402
  81.5 0.0 collective-permute-done.16
  81.5 3.1 %collective-permute-done.17 = f32[32,64]{1,0:T(8,128)S(1)} collective-permute-done((f32[32,64]{1,0:T(8,128)S(1)}, f32[32,64]{1,0:T(8,128)S(1)}, u32[]{:S(2)}, u32[]{:S(2)}) %collective-permute-start.17) | collective-permute-done | bytes 8224 | tf_op jit(solution)/shard_map/ppermute | solution.py:402
  84.7 0.6 add_add_fusion
  (2 shorter events, 0.0 us)
Async XLA Ops:
  1.6 22.0 %collective-permute-start.1 = (bf16[1280,640]{1,0:T(8,128)(2,1)S(1)}, bf16[1280,640]{1,0:T(8,128)(2,1)S(1)}, u32[]{:S(2)}, u32[]{:S(2)}) collective-permute-start(bf16[1280,640]{1,0:T(8,128)(2,1)S(1)} %get-tuple-element.13.mine_pack), channel_id=1, source_target_pairs={{0,4},{4,0},{8,12},{12,8},{16,20},{20,16},{24,28},{28,24},{32,36},... | collective-permute-start | bytes 4915208 | tf_op jit(solution)/shard_map/ppermute | solution.py:375
  1.7 7.8 %collective-permute-start.2 = (bf16[128,640]{1,0:T(8,128)(2,1)S(1)}, bf16[128,640]{1,0:T(8,128)(2,1)S(1)}, u32[]{:S(2)}, u32[]{:S(2)}) collective-permute-start(bf16[128,640]{1,0:T(8,128)(2,1)S(1)} %get-tuple-element.12.here), channel_id=1, source_target_pairs={{0,8},{4,12},{8,16},{12,20},{16,24},{20,28},{24,0},{28,4},{32,40},... | collective-permute-start | bytes 491528 | tf_op jit(solution)/shard_map/ppermute | solution.py:378
  3.3 6.4 %collective-permute-start = (bf16[128,640]{1,0:T(8,128)(2,1)S(1)}, bf16[128,640]{1,0:T(8,128)(2,1)S(1)}, u32[]{:S(2)}, u32[]{:S(2)}) collective-permute-start(bf16[128,640]{1,0:T(8,128)(2,1)S(1)} %get-tuple-element.12.here), channel_id=1, source_target_pairs={{0,32},{4,36},{8,40},{12,44},{16,48},{20,52},{24,56},{28,60},{32,0... | collective-permute-start | bytes 491528 | tf_op jit(solution)/shard_map/ppermute | solution.py:376
  5.2 6.0 %collective-permute-start.3 = (bf16[128,640]{1,0:T(8,128)(2,1)S(1)}, bf16[128,640]{1,0:T(8,128)(2,1)S(1)}, u32[]{:S(2)}, u32[]{:S(2)}) collective-permute-start(bf16[128,640]{1,0:T(8,128)(2,1)S(1)} %get-tuple-element.12.here), channel_id=1, source_target_pairs={{0,24},{4,28},{8,0},{12,4},{16,8},{20,12},{24,16},{28,20},{32,56},... | collective-permute-start | bytes 491528 | tf_op jit(solution)/shard_map/ppermute | solution.py:378
  11.2 5.9 %collective-permute-start.6 = (bf16[128,640]{1,0:T(8,128)(2,1)S(1)}, bf16[128,640]{1,0:T(8,128)(2,1)S(1)}, u32[]{:S(2)}, u32[]{:S(2)}) collective-permute-start(bf16[128,640]{1,0:T(8,128)(2,1)S(1)} %hold.1), channel_id=1, source_target_pairs={{0,24},{4,28},{8,0},{12,4},{16,8},{20,12},{24,16},{28,20},{32,56},... | collective-permute-start | bytes 491528 | tf_op jit(solution)/shard_map/ppermute | solution.py:380
  14.2 6.5 %collective-permute-start.8 = (bf16[128,640]{1,0:T(8,128)(2,1)S(1)}, bf16[128,640]{1,0:T(8,128)(2,1)S(1)}, u32[]{:S(2)}, u32[]{:S(2)}) collective-permute-start(bf16[128,640]{1,0:T(8,128)(2,1)S(1)} %collective-permute-done.2.rest_0_.here), channel_id=1, source_target_pairs={{0,8},{4,12},{8,16},{12,20},{16,24},{20,28},{24,0},{28,4},{32,40},... | collective-permute-start | bytes 491528 | tf_op jit(solution)/shard_map/ppermute | solution.py:385
  17.1 6.5 %collective-permute-start.9 = (bf16[128,640]{1,0:T(8,128)(2,1)S(1)}, bf16[128,640]{1,0:T(8,128)(2,1)S(1)}, u32[]{:S(2)}, u32[]{:S(2)}) collective-permute-start(bf16[128,640]{1,0:T(8,128)(2,1)S(1)} %collective-permute-done.6.there), channel_id=1, source_target_pairs={{0,24},{4,28},{8,0},{12,4},{16,8},{20,12},{24,16},{28,20},{32,56},... | collective-permute-start | bytes 491528 | tf_op jit(solution)/shard_map/ppermute | solution.py:385
  20.7 12.9 %collective-permute-start.4 = (bf16[128,640]{1,0:T(8,128)(2,1)S(1)}, bf16[128,640]{1,0:T(8,128)(2,1)S(1)}, u32[]{:S(2)}, u32[]{:S(2)}) collective-permute-start(bf16[128,640]{1,0:T(8,128)(2,1)S(1)} %hold.1), channel_id=1, source_target_pairs={{0,8},{4,12},{8,16},{12,20},{16,24},{20,28},{24,0},{28,4},{32,40},... | collective-permute-start | bytes 491528 | tf_op jit(solution)/shard_map/ppermute | solution.py:380
  26.2 13.3 %collective-permute-start.10 = (bf16[1312,128]{1,0:T(8,128)(2,1)S(1)}, bf16[1312,128]{1,0:T(8,128)(2,1)S(1)}, u32[]{:S(2)}, u32[]{:S(2)}) collective-permute-start(bf16[1312,128]{1,0:T(8,128)(2,1)S(1)} %attend.7), channel_id=1, source_target_pairs={{0,16},{4,20},{8,24},{12,28},{16,0},{20,4},{24,8},{28,12},{32,48},... | collective-permute-start | bytes 1007624 | tf_op jit(solution)/shard_map/ppermute | solution.py:392
  28.2 20.9 %slice-start = ((s8[6553600]{0:T(1024)(128)(4,1)}), s8[4194304]{0:T(1024)(128)(4,1)S(1)}, s32[]{:S(2)}) async-start(s8[6553600]{0:T(1024)(128)(4,1)} %bitcast.6), calls=%async_computation | async-start | bytes 8388608
  30.7 18.3 %slice-start.1 = ((s8[6553600]{0:T(1024)(128)(4,1)}), s8[2359296]{0:T(1024)(128)(4,1)S(1)}, s32[]{:S(2)}) async-start(s8[6553600]{0:T(1024)(128)(4,1)} %bitcast.6), calls=%async_computation.1 | async-start | bytes 4718592
  30.8 11.4 %collective-permute-start.7 = (bf16[1312,128]{1,0:T(8,128)(2,1)S(1)}, bf16[1312,128]{1,0:T(8,128)(2,1)S(1)}, u32[]{:S(2)}, u32[]{:S(2)}) collective-permute-start(bf16[1312,128]{1,0:T(8,128)(2,1)S(1)} %attend.6), channel_id=1, source_target_pairs={{0,8},{4,12},{8,16},{12,20},{16,24},{20,28},{24,0},{28,4},{32,40},... | collective-permute-start | bytes 1007624 | tf_op jit(solution)/shard_map/ppermute | solution.py:392
  36.2 7.2 %collective-permute-start.5 = (bf16[1312,128]{1,0:T(8,128)(2,1)S(1)}, bf16[1312,128]{1,0:T(8,128)(2,1)S(1)}, u32[]{:S(2)}, u32[]{:S(2)}) collective-permute-start(bf16[1312,128]{1,0:T(8,128)(2,1)S(1)} %attend.5), channel_id=1, source_target_pairs={{0,24},{4,28},{8,0},{12,4},{16,8},{20,12},{24,16},{28,20},{32,56},... | collective-permute-start | bytes 1007624 | tf_op jit(solution)/shard_map/ppermute | solution.py:392
  43.6 5.5 %collective-permute-start.11 = (bf16[656,128]{1,0:T(8,128)(2,1)S(1)}, bf16[656,128]{1,0:T(8,128)(2,1)S(1)}, u32[]{:S(2)}, u32[]{:S(2)}) collective-permute-start(bf16[656,128]{1,0:T(8,128)(2,1)S(1)} %merge.1), channel_id=1, source_target_pairs={{0,32},{4,36},{8,40},{12,44},{16,48},{20,52},{24,56},{28,60},{32,0... | collective-permute-start | bytes 503816 | tf_op jit(solution)/shard_map/ppermute | solution.py:393
  51.2 23.1 %copy-start = (f32[32,2,5120]{2,1,0:T(2,128)S(1)}, f32[32,2,5120]{2,1,0:T(2,128)}, u32[]{:S(2)}) copy-start(f32[32,2,5120]{2,1,0:T(2,128)} %table.1) | copy-start | bytes 3932164
  51.2 23.1 %copy-start.1 = (bf16[1,32,5120]{2,1,0:T(8,128)(2,1)S(1)}, bf16[1,32,5120]{2,1,0:T(8,128)(2,1)}, u32[]{:S(2)}) copy-start(bf16[1,32,5120]{2,1,0:T(8,128)(2,1)} %param.22) | copy-start | bytes 983044
  51.2 23.1 %copy-start.2 = (s32[4]{0:T(128)S(1)}, s32[4]{0:T(128)}, u32[]{:S(2)}) copy-start(s32[4]{0:T(128)} %group_branch.3) | copy-start | bytes 52
  51.2 23.1 %copy-start.3 = (f32[4]{0:T(128)S(1)}, f32[4]{0:T(128)}, u32[]{:S(2)}) copy-start(f32[4]{0:T(128)} %guidance_w.1) | copy-start | bytes 52
  51.2 23.1 %copy-start.4 = (s32[32]{0:T(128)S(1)}, s32[32]{0:T(128)}, u32[]{:S(2)}) copy-start(s32[32]{0:T(128)} %frame_level.1) | copy-start | bytes 388
  51.2 13.7 %collective-permute-start.13 = (bf16[32,5120]{1,0:T(8,128)(2,1)S(1)}, bf16[32,5120]{1,0:T(8,128)(2,1)S(1)}, u32[]{:S(2)}, u32[]{:S(2)}) collective-permute-start(bf16[32,5120]{1,0:T(8,128)(2,1)S(1)} %get-tuple-element.18), channel_id=1, source_target_pairs={{0,3},{4,7},{8,11},{12,15},{16,19},{20,23},{24,27},{28,31},{1,0},{... | collective-permute-start | bytes 983048 | tf_op jit(solution)/shard_map/ppermute | solution.py:395
  56.7 13.3 %collective-permute-start.12 = (bf16[32,5120]{1,0:T(8,128)(2,1)}, bf16[32,5120]{1,0:T(8,128)(2,1)}, u32[]{:S(2)}, u32[]{:S(2)}) collective-permute-start(bf16[32,5120]{1,0:T(8,128)(2,1)} %get-tuple-element.16), channel_id=1, source_target_pairs={{0,3},{4,7},{8,11},{12,15},{16,19},{20,23},{24,27},{28,31},{1,0},{... | collective-permute-start | bytes 983048 | tf_op jit(solution)/shard_map/ppermute | solution.py:396
  65.7 8.6 %collective-permute-start.14 = (bf16[32,5120]{1,0:T(8,128)(2,1)}, bf16[32,5120]{1,0:T(8,128)(2,1)}, u32[]{:S(2)}, u32[]{:S(2)}) collective-permute-start(bf16[32,5120]{1,0:T(8,128)(2,1)} %add_convert_fusion), channel_id=1, source_target_pairs={{0,35},{4,39},{8,43},{12,47},{16,51},{20,55},{24,59},{28,63},{1,32... | collective-permute-start | bytes 983048 | tf_op jit(solution)/shard_map/ppermute | solution.py:398
  76.2 5.3 %collective-permute-start.15 = (f32[32,64]{1,0:T(8,128)S(1)}, f32[32,64]{1,0:T(8,128)S(1)}, u32[]{:S(2)}, u32[]{:S(2)}) collective-permute-start(f32[32,64]{1,0:T(8,128)S(1)} %head.1), channel_id=1, source_target_pairs={{0,128},{64,192},{128,0},{192,64},{1,129},{65,193},{129,1},{193,65... | collective-permute-start | bytes 24584 | tf_op jit(solution)/shard_map/ppermute | solution.py:402
  77.5 4.0 %collective-permute-start.16 = (f32[32,64]{1,0:T(8,128)S(1)}, f32[32,64]{1,0:T(8,128)S(1)}, u32[]{:S(2)}, u32[]{:S(2)}) collective-permute-start(f32[32,64]{1,0:T(8,128)S(1)} %head.1), channel_id=1, source_target_pairs={{0,64},{64,128},{128,192},{192,0},{1,65},{65,129},{129,193},{193,1... | collective-permute-start | bytes 24584 | tf_op jit(solution)/shard_map/ppermute | solution.py:402
  79.7 4.9 %collective-permute-start.17 = (f32[32,64]{1,0:T(8,128)S(1)}, f32[32,64]{1,0:T(8,128)S(1)}, u32[]{:S(2)}, u32[]{:S(2)}) collective-permute-start(f32[32,64]{1,0:T(8,128)S(1)} %head.1), channel_id=1, source_target_pairs={{0,192},{64,0},{128,64},{192,128},{1,193},{65,1},{129,65},{193,129... | collective-permute-start | bytes 24584 | tf_op jit(solution)/shard_map/ppermute | solution.py:402

commit v4 on v3

--- a/solution.py
+++ b/solution.py
@@ -158,20 +158,30 @@
     )
 
 
-def attend_kernel(here, there, mine_pack, core_pack, bias, *rest):
-    sent = rest[-1]
+def attend_kernel(joins, first, second, mine_pack, core_pack, bias, *rest):
     packs = (mine_pack, core_pack)
-    rows, feat = here.shape
-    half = rows // 2
+    sent = rest[-2:]
+    rows, feat = first.shape
+    height = feat + STAT_ROWS
     heads = feat // HSZ
     count = mine_pack.shape[0] - feat
     levels = []
 
+    def put(at, value):
+        size = value.shape[0]
+        for i in range(2):
+            got = value[:, i * rows : (i + 1) * rows]
+            if joins:
+                partner = rest[i][at : at + size, :]
+                low = lax.broadcasted_iota(jnp.int32, got.shape, 1) < rows // 2
+                sent[i][at : at + size, :] = jnp.where(low, partner, got)
+                sent[i][height + at : height + at + size, :] = jnp.where(low, got, partner)
+            else:
+                sent[i][at : at + size, :] = got
+
     def scores_of(h):
         cols = slice(h * HSZ, (h + 1) * HSZ)
-        q = jnp.concatenate(
-            [there[half:, cols], here[:half, cols], here[half:, cols], there[:half, cols]], axis=0
-        )
+        q = jnp.concatenate([first[:, cols], second[:, cols]], axis=0)
         scores = []
         for i, pack_ref in enumerate(packs):
             s = lax.dot_general(
@@ -199,15 +209,9 @@
                 weights.astype(jnp.bfloat16),
                 preferred_element_type=jnp.float32,
             )
-        out = (summed / total).astype(jnp.bfloat16)
-        for i in range(2):
-            start = i * (feat + STAT_ROWS) + h * HSZ
-            sent[start : start + HSZ, :] = out[:, i * rows : (i + 1) * rows]
+        put(h * HSZ, (summed / total).astype(jnp.bfloat16))
         levels.append(peak * SCORE_TO_EXP2 + jnp.log2(total))
-    stats = stat_rows(levels)
-    for i in range(2):
-        start = i * (feat + STAT_ROWS) + feat
-        sent[start : start + STAT_ROWS, :] = stats[:, i * rows : (i + 1) * rows]
+    put(feat, stat_rows(levels))
 
 
 def stat_rows(levels):
@@ -218,15 +222,16 @@
     return jnp.concatenate([high, middle, level - high - middle, spare], axis=0).astype(jnp.bfloat16)
 
 
-def attend(queries, packs, bias, after):
-    rows, feat = queries[0].shape
+def attend(blocks, packs, bias, partners=(), after=()):
+    rows, feat = blocks[0].shape
     count = packs[0].shape[0] - feat
-    vmem = pl.BlockSpec(memory_space=pltpu.VMEM)
-    return pl.pallas_call(
-        attend_kernel,
-        out_shape=jax.ShapeDtypeStruct((2 * (feat + STAT_ROWS), rows), jnp.bfloat16),
-        in_specs=[vmem] * 5 + [pl.BlockSpec(memory_space=pl.ANY)] * len(after),
-        out_specs=vmem,
+    height = (feat + STAT_ROWS) * (2 if partners else 1)
+    vmem = pl.BlockSpec(memory_space=pltpu.VMEM)
+    return pl.pallas_call(
+        functools.partial(attend_kernel, bool(partners)),
+        out_shape=[jax.ShapeDtypeStruct((height, rows), jnp.bfloat16)] * 2,
+        in_specs=[vmem] * (5 + len(partners)) + [pl.BlockSpec(memory_space=pl.ANY)] * len(after),
+        out_specs=[vmem] * 2,
         compiler_params=pltpu.CompilerParams(vmem_limit_bytes=16 * 2**20),
         cost_estimate=pl.CostEstimate(
             flops=16 * rows * count * feat,
@@ -234,7 +239,7 @@
             transcendentals=4 * rows * count * (feat // HSZ),
         ),
         name="attend",
-    )(*queries, *packs, bias, *after)
+    )(*blocks, *packs, bias, *partners, *after)
 
 
 def merged(parts, heads):
@@ -316,6 +321,22 @@
         ),
         name="project",
     )(*parts, weight)
+
+
+def add_kernel(first, second, out):
+    out[...] = (first[...].astype(jnp.float32) + second[...].astype(jnp.float32)).astype(out.dtype)
+
+
+def add(first, second):
+    vmem = pl.BlockSpec(memory_space=pltpu.VMEM)
+    return pl.pallas_call(
+        add_kernel,
+        out_shape=jax.ShapeDtypeStruct(first.shape, first.dtype),
+        in_specs=[vmem] * 2,
+        out_specs=vmem,
+        compiler_params=pltpu.CompilerParams(vmem_limit_bytes=4 * 2**20),
+        name="add",
+    )(first, second)
 
 
 def head_kernel(
@@ -378,23 +399,23 @@
     mine_up, mine_down = lax.ppermute(mine, "seq", up), lax.ppermute(mine, "seq", down)
     ready = hold(across, [mine_up, mine_down])
     across_up, across_down = lax.ppermute(ready, "seq", up), lax.ppermute(ready, "seq", down)
-    pairs = {
-        0: (mine, across),
-        1: (mine_up, across_up),
-        3: (mine_down, across_down),
-        2: (lax.ppermute(mine_up, "seq", up), lax.ppermute(across_down, "seq", down)),
-    }
-    parts = []
-    made = []
-    for dx in (0, 1, 3, 2):
-        sent = attend(pairs[dx], packs, bias, ())
-        made.append(sent)
-        parts.append(lax.ppermute(sent, "seq", hop(0, -dx, 0)) if dx else sent)
+    mine_two = lax.ppermute(mine_up, "seq", up)
+    across_two = lax.ppermute(ready, "seq", hop(0, 2, 0))
+    out_up, out_down = attend((mine_up, mine_down), packs, bias)
+    out_two, out_own = attend((mine_two, mine), packs, bias)
+    sent_up, sent_down = attend((across_up, across_down), packs, bias, (out_up, out_down))
+    sent_two, sent_own = attend((across_two, across), packs, bias, (out_two, out_own))
+    parts = [
+        lax.ppermute(sent_up, "seq", down),
+        lax.ppermute(sent_down, "seq", up),
+        lax.ppermute(sent_two, "seq", hop(0, 2, 0)),
+        sent_own,
+    ]
     parts.append(lax.ppermute(merge(parts), "seq", hop(1, 0, 0)))
-    near_block, far_block, side_block, own_block = project(parts, out_weight)
+    side_block, own_block, near_block, far_block = project(parts, out_weight)
     passed = lax.ppermute(far_block, ("seq", "mp"), pair_hop(onward))
     aside = lax.ppermute(side_block, ("seq", "mp"), pair_hop(onward))
-    joined = (near_block.astype(jnp.float32) + passed.astype(jnp.float32)).astype(jnp.bfloat16)
+    joined = add(near_block, passed)
     reduced = [own_block, aside, lax.ppermute(joined, ("seq", "mp"), pair_hop(across_onward))]
     velocity = head(
         group_branch, guidance_w, frame_level, reduced, residual[0], mod_table, head_weight

time: 85.4 us -> 85 us (level)
  Pallas kernels: 16 us -> 16.9 us
    ppermute x5, waiting for transfers between devices: 6.82 us -> 11.6 us  [the longest x1 3.49 us: body(): lax.ppermute(sent_two, 'seq', hop(0, 2, 0))]
    ppermute x5, starting transfers between devices: 9.26 us -> 5.47 us  [the longest x1 2.82 us: body(): across_two = lax.ppermute(ready, 'seq', hop(0, 2, 0))]
    ppermute x1, waiting for transfers between devices: 2.83 us -> 0.01 us  [body(): lax.ppermute(ready, 'seq', down)]
    ppermute x1, starting transfers between devices: 0.39 us -> 2.77 us  [body(): parts.append(lax.ppermute(merge(parts), 'seq', hop(1, 0, 0)))]
    ppermute x1, waiting for transfers between devices: 5.06 us -> 3.34 us  [body(): parts.append(lax.ppermute(merge(parts), 'seq', hop(1, 0, 0)))]
    ppermute x1, starting transfers between devices: 0.01 us -> 1.08 us  [body(): lax.ppermute(ready, 'seq', up)]
    ppermute x1, starting transfers between devices: 3.03 us -> 2.15 us  [body(): lax.ppermute(ready, 'seq', down)]
    pallas_call x4 -> x5, Pallas kernels: 10.3 us -> 11.1 us  [the longest x4 10.3 us: attend(): pl.pallas_call(functools.partial(attend_kernel, bool(partners)), out_shap...]
  transfers between devices with their start and end apart: 18 -> 18, of which waited for: 12 -> 11; matrix products, arithmetic and copies ran while one was open for 3% -> 2% of each run, Pallas kernels for 12% -> 13%
where the time goes in v4:
time: 85 us; the launch traced here: 84.8 us
  waiting for transfers between devices  34.5 us (41%)
  starting transfers between devices  30.9 us (36%)
  Pallas kernels  16.9 us (20%)
  local copies, waits for them, and re-layouts  1.69 us (2%)
    pallas_call x4, Pallas kernels, attend(): pl.pallas_call(functools.partial(attend_kernel, bool(partners)), out_shap...  10.3 us
    ppermute x1, waiting for transfers between devices, body(): passed = lax.ppermute(far_block, ('seq', 'mp'), pair_hop(onward))  6.71 us
    ppermute x1, starting transfers between devices, body(): passed = lax.ppermute(far_block, ('seq', 'mp'), pair_hop(onward))  6.23 us
    ppermute x3, waiting for transfers between devices, body(): around = [lax.ppermute(velocity, 'branch', turn(k)) for k in (1, 3, 2)]  4.95 us
    ppermute x1, waiting for transfers between devices, body(): lax.ppermute(joined, ('seq', 'mp'), pair_hop(across_onward))  3.99 us
    ppermute x3, starting transfers between devices, body(): around = [lax.ppermute(velocity, 'branch', turn(k)) for k in (1, 3, 2)]  3.51 us
    ppermute x1, waiting for transfers between devices, body(): lax.ppermute(sent_two, 'seq', hop(0, 2, 0))  3.49 us
    ppermute x1, waiting for transfers between devices, body(): parts.append(lax.ppermute(merge(parts), 'seq', hop(1, 0, 0)))  3.34 us
  transfers between devices with their start and end apart: 18, of which 11 were waited for; matrix products, arithmetic and copies ran while one was open for 2% of the time, Pallas kernels for 13%

profile of v4, /device:TPU:24, one launch (start us, length us, event | category | flops | bytes accessed | tf_op | source)
XLA Modules:
  0.0 84.8 jit_solution(10377334029607871123)
XLA Ops:
  0.0 1.6 %pack.1 = (bf16[1280,640]{1,0:T(8,128)(2,1)S(1)}, f32[1280,128]{1,0:T(8,128)S(1)}, bf16[128,640]{1,0:T(8,128)(2,1)S(1)}) custom-call(bf16[128,640]{1,0:T(8,128)(2,1)} %bitcast.11, bf16[128,640]{1,0:T(8,128)(2,1)} %bitcast.12, bf16[128,640]{1,0:T(8,128)(2,1)} %bitcast.13, bf16[512,640]{1,0:T(8,128)(2,1)} %bitcast.9, bf16[512,640]{1,0:T(8,128)(2,1)} %bitcast.10, ...), custom_call_target="tpu_custom_call" | custom-call | flops 6000000000 | bytes 1638400 | tf_op jit(solution)/shard_map/pack/pallas_call | solution.py:133
  1.6 0.1 collective-permute-start.5
  1.7 1.6 %collective-permute-start.1 = (bf16[128,640]{1,0:T(8,128)(2,1)S(1)}, bf16[128,640]{1,0:T(8,128)(2,1)S(1)}, u32[]{:S(2)}, u32[]{:S(2)}) collective-permute-start(bf16[128,640]{1,0:T(8,128)(2,1)S(1)} %get-tuple-element.20.second), channel_id=1, source_target_pairs={{0,8},{4,12},{8,16},{12,20},{16,24},{20,28},{24,0},{28,4},{32,40},... | collective-permute-start | bytes 491528 | tf_op jit(solution)/shard_map/ppermute | solution.py:399
  3.3 1.9 %collective-permute-start = (bf16[128,640]{1,0:T(8,128)(2,1)S(1)}, bf16[128,640]{1,0:T(8,128)(2,1)S(1)}, u32[]{:S(2)}, u32[]{:S(2)}) collective-permute-start(bf16[128,640]{1,0:T(8,128)(2,1)S(1)} %get-tuple-element.20.second), channel_id=1, source_target_pairs={{0,32},{4,36},{8,40},{12,44},{16,48},{20,52},{24,56},{28,60},{32,0... | collective-permute-start | bytes 491528 | tf_op jit(solution)/shard_map/ppermute | solution.py:397
  5.2 1.7 %collective-permute-start.2 = (bf16[128,640]{1,0:T(8,128)(2,1)S(1)}, bf16[128,640]{1,0:T(8,128)(2,1)S(1)}, u32[]{:S(2)}, u32[]{:S(2)}) collective-permute-start(bf16[128,640]{1,0:T(8,128)(2,1)S(1)} %get-tuple-element.20.second), channel_id=1, source_target_pairs={{0,24},{4,28},{8,0},{12,4},{16,8},{20,12},{24,16},{28,20},{32,56},... | collective-permute-start | bytes 491528 | tf_op jit(solution)/shard_map/ppermute | solution.py:399
  6.9 2.6 %collective-permute-done.1.rest_0_.first = bf16[128,640]{1,0:T(8,128)(2,1)S(1)} collective-permute-done((bf16[128,640]{1,0:T(8,128)(2,1)S(1)}, bf16[128,640]{1,0:T(8,128)(2,1)S(1)}, u32[]{:S(2)}, u32[]{:S(2)}) %collective-permute-start.1) | collective-permute-done | bytes 163872 | tf_op jit(solution)/shard_map/ppermute | solution.py:399
  9.5 0.3 collective-permute-start.9
  9.8 0.0 collective-permute-done.source.second
  9.8 1.4 %collective-permute-done.2.rest_1_.second = bf16[128,640]{1,0:T(8,128)(2,1)S(1)} collective-permute-done((bf16[128,640]{1,0:T(8,128)(2,1)S(1)}, bf16[128,640]{1,0:T(8,128)(2,1)S(1)}, u32[]{:S(2)}, u32[]{:S(2)}) %collective-permute-start.2) | collective-permute-done | bytes 163872 | tf_op jit(solution)/shard_map/ppermute | solution.py:399
  11.2 2.8 %collective-permute-start.8 = (bf16[128,640]{1,0:T(8,128)(2,1)S(1)}, bf16[128,640]{1,0:T(8,128)(2,1)S(1)}, u32[]{:S(2)}, u32[]{:S(2)}) collective-permute-start(bf16[128,640]{1,0:T(8,128)(2,1)S(1)} %hold.1), channel_id=1, source_target_pairs={{0,16},{4,20},{8,24},{12,28},{16,0},{20,4},{24,8},{28,12},{32,48},... | collective-permute-start | bytes 491528 | tf_op jit(solution)/shard_map/ppermute | solution.py:403
  14.0 1.1 %collective-permute-start.3 = (bf16[128,640]{1,0:T(8,128)(2,1)S(1)}, bf16[128,640]{1,0:T(8,128)(2,1)S(1)}, u32[]{:S(2)}, u32[]{:S(2)}) collective-permute-start(bf16[128,640]{1,0:T(8,128)(2,1)S(1)} %hold.1), channel_id=1, source_target_pairs={{0,8},{4,12},{8,16},{12,20},{16,24},{20,28},{24,0},{28,4},{32,40},... | collective-permute-start | bytes 491528 | tf_op jit(solution)/shard_map/ppermute | solution.py:401
  15.1 2.2 %collective-permute-start.4 = (bf16[128,640]{1,0:T(8,128)(2,1)S(1)}, bf16[128,640]{1,0:T(8,128)(2,1)S(1)}, u32[]{:S(2)}, u32[]{:S(2)}) collective-permute-start(bf16[128,640]{1,0:T(8,128)(2,1)S(1)} %hold.1), channel_id=1, source_target_pairs={{0,24},{4,28},{8,0},{12,4},{16,8},{20,12},{24,16},{28,20},{32,56},... | collective-permute-start | bytes 491528 | tf_op jit(solution)/shard_map/ppermute | solution.py:401
  17.2 3.0 %collective-permute-done.9.first = bf16[128,640]{1,0:T(8,128)(2,1)S(1)} collective-permute-done((bf16[128,640]{1,0:T(8,128)(2,1)S(1)}, bf16[128,640]{1,0:T(8,128)(2,1)S(1)}, u32[]{:S(2)}, u32[]{:S(2)}) %collective-permute-start.9) | collective-permute-done | bytes 163872 | tf_op jit(solution)/shard_map/ppermute | solution.py:402
  20.3 0.0 collective-permute-done.5.core_pack
  20.3 2.6 %attend.6 = (bf16[656,128]{1,0:T(8,128)(2,1)S(1)}, bf16[656,128]{1,0:T(8,128)(2,1)S(1)}) custom-call(bf16[128,640]{1,0:T(8,128)(2,1)S(1)} %collective-permute-done.9.first, bf16[128,640]{1,0:T(8,128)(2,1)S(1)} %get-tuple-element.20.second, bf16[1280,640]{1,0:T(8,128)(2,1)S(1)} %get-tuple-element.21.mine_pack, ...), custom_call_target="tpu_custom_call" | custom-call | flops 838860800 | bytes 3276800 | tf_op jit(solution)/shard_map/attend/pallas_call | solution.py:230
  22.8 0.0 collective-permute-done.8.first
  22.8 0.0 slice-start
  22.9 2.6 %attend.7 = (bf16[1312,128]{1,0:T(8,128)(2,1)S(1)}, bf16[1312,128]{1,0:T(8,128)(2,1)S(1)}) custom-call(bf16[128,640]{1,0:T(8,128)(2,1)S(1)} %collective-permute-done.8.first, bf16[128,640]{1,0:T(8,128)(2,1)S(1)} %collective-permute-done.source.second, bf16[1280,640]{1,0:T(8,128)(2,1)S(1)} %get-tuple-element.21.mine_pack, ...), custom_call_target="tpu_custom_call" | custom-call | flops 838860800 | bytes 3276800 | tf_op jit(solution)/shard_map/attend/pallas_call | solution.py:230
  25.5 0.0 slice-start.1
  25.5 0.3 collective-permute-start.10
  25.8 2.6 %attend.4 = (bf16[656,128]{1,0:T(8,128)(2,1)S(1)}, bf16[656,128]{1,0:T(8,128)(2,1)S(1)}) custom-call(bf16[128,640]{1,0:T(8,128)(2,1)S(1)} %collective-permute-done.1.rest_0_.first, bf16[128,640]{1,0:T(8,128)(2,1)S(1)} %collective-permute-done.2.rest_1_.second, bf16[1280,640]{1,0:T(8,128)(2,1)S(1)} %get-tuple-element.21.mine_pack, ...), custom_call_target="tpu_custom_call" | custom-call | flops 838860800 | bytes 3276800 | tf_op jit(solution)/shard_map/attend/pallas_call | solution.py:230
  28.3 0.0 collective-permute-done.3.first
  28.4 0.0 collective-permute-done.4.second
  28.4 2.6 %attend.5 = (bf16[1312,128]{1,0:T(8,128)(2,1)S(1)}, bf16[1312,128]{1,0:T(8,128)(2,1)S(1)}) custom-call(bf16[128,640]{1,0:T(8,128)(2,1)S(1)} %collective-permute-done.3.first, bf16[128,640]{1,0:T(8,128)(2,1)S(1)} %collective-permute-done.4.second, bf16[1280,640]{1,0:T(8,128)(2,1)S(1)} %get-tuple-element.21.mine_pack, ...), custom_call_target="tpu_custom_call" | custom-call | flops 838860800 | bytes 3276800 | tf_op jit(solution)/shard_map/attend/pallas_call | solution.py:230
  31.0 1.0 %collective-permute-start.6 = (bf16[1312,128]{1,0:T(8,128)(2,1)S(1)}, bf16[1312,128]{1,0:T(8,128)(2,1)S(1)}, u32[]{:S(2)}, u32[]{:S(2)}) collective-permute-start(bf16[1312,128]{1,0:T(8,128)(2,1)S(1)} %get-tuple-element.25), channel_id=1, source_target_pairs={{0,24},{4,28},{8,0},{12,4},{16,8},{20,12},{24,16},{28,20},{32,56},... | collective-permute-start | bytes 1007624 | tf_op jit(solution)/shard_map/ppermute | solution.py:409
  32.0 1.1 %collective-permute-start.7 = (bf16[1312,128]{1,0:T(8,128)(2,1)S(1)}, bf16[1312,128]{1,0:T(8,128)(2,1)S(1)}, u32[]{:S(2)}, u32[]{:S(2)}) collective-permute-start(bf16[1312,128]{1,0:T(8,128)(2,1)S(1)} %get-tuple-element.26), channel_id=1, source_target_pairs={{0,8},{4,12},{8,16},{12,20},{16,24},{20,28},{24,0},{28,4},{32,40},... | collective-permute-start | bytes 1007624 | tf_op jit(solution)/shard_map/ppermute | solution.py:410
  33.1 3.5 %collective-permute-done.10.refs_2_ = bf16[1312,128]{1,0:T(8,128)(2,1)S(1)} collective-permute-done((bf16[1312,128]{1,0:T(8,128)(2,1)S(1)}, bf16[1312,128]{1,0:T(8,128)(2,1)S(1)}, u32[]{:S(2)}, u32[]{:S(2)}) %collective-permute-start.10) | collective-permute-done | bytes 335904 | tf_op jit(solution)/shard_map/ppermute | solution.py:411
  36.6 2.2 %collective-permute-done.6.refs_0_ = bf16[1312,128]{1,0:T(8,128)(2,1)S(1)} collective-permute-done((bf16[1312,128]{1,0:T(8,128)(2,1)S(1)}, bf16[1312,128]{1,0:T(8,128)(2,1)S(1)}, u32[]{:S(2)}, u32[]{:S(2)}) %collective-permute-start.6) | collective-permute-done | bytes 335904 | tf_op jit(solution)/shard_map/ppermute | solution.py:409
  38.8 2.8 %collective-permute-done.7.refs_1_ = bf16[1312,128]{1,0:T(8,128)(2,1)S(1)} collective-permute-done((bf16[1312,128]{1,0:T(8,128)(2,1)S(1)}, bf16[1312,128]{1,0:T(8,128)(2,1)S(1)}, u32[]{:S(2)}, u32[]{:S(2)}) %collective-permute-start.7) | collective-permute-done | bytes 335904 | tf_op jit(solution)/shard_map/ppermute | solution.py:410
  41.6 0.2 merge.1
  41.8 2.8 %collective-permute-start.11 = (bf16[656,128]{1,0:T(8,128)(2,1)S(1)}, bf16[656,128]{1,0:T(8,128)(2,1)S(1)}, u32[]{:S(2)}, u32[]{:S(2)}) collective-permute-start(bf16[656,128]{1,0:T(8,128)(2,1)S(1)} %merge.1), channel_id=1, source_target_pairs={{0,32},{4,36},{8,40},{12,44},{16,48},{20,52},{24,56},{28,60},{32,0... | collective-permute-start | bytes 503816 | tf_op jit(solution)/shard_map/ppermute | solution.py:414
  44.6 3.3 %collective-permute-done.11.refs_4_ = bf16[656,128]{1,0:T(8,128)(2,1)S(1)} collective-permute-done((bf16[656,128]{1,0:T(8,128)(2,1)S(1)}, bf16[656,128]{1,0:T(8,128)(2,1)S(1)}, u32[]{:S(2)}, u32[]{:S(2)}) %collective-permute-start.11) | collective-permute-done | bytes 167968 | tf_op jit(solution)/shard_map/ppermute | solution.py:414
  47.9 0.0 slice-done
  47.9 0.0 slice-done.1
  47.9 2.1 %project.1 = (bf16[32,5120]{1,0:T(8,128)(2,1)}, bf16[32,5120]{1,0:T(8,128)(2,1)S(1)}, bf16[32,5120]{1,0:T(8,128)(2,1)S(1)}, bf16[32,5120]{1,0:T(8,128)(2,1)S(1)}) custom-call(bf16[1312,128]{1,0:T(8,128)(2,1)S(1)} %collective-permute-done.6.refs_0_, bf16[1312,128]{1,0:T(8,128)(2,1)S(1)} %collective-permute-done.7.refs_1_, ...), custom_call_target="tpu_custom_call" | custom-call | flops 838860800 | bytes 6553600 | tf_op jit(solution)/shard_map/project/pallas_call | solution.py:312
  50.0 0.0 copy-start
  50.0 0.0 copy-start.1
  50.0 0.0 copy-start.2
  50.0 0.0 copy-start.3
  50.0 0.0 copy-start.4
  50.0 6.2 %collective-permute-start.13 = (bf16[32,5120]{1,0:T(8,128)(2,1)S(1)}, bf16[32,5120]{1,0:T(8,128)(2,1)S(1)}, u32[]{:S(2)}, u32[]{:S(2)}) collective-permute-start(bf16[32,5120]{1,0:T(8,128)(2,1)S(1)} %get-tuple-element.34), channel_id=1, source_target_pairs={{0,3},{4,7},{8,11},{12,15},{16,19},{20,23},{24,27},{28,31},{1,0},{... | collective-permute-start | bytes 983048 | tf_op jit(solution)/shard_map/ppermute | solution.py:416
  56.2 1.5 %collective-permute-start.12 = (bf16[32,5120]{1,0:T(8,128)(2,1)}, bf16[32,5120]{1,0:T(8,128)(2,1)}, u32[]{:S(2)}, u32[]{:S(2)}) collective-permute-start(bf16[32,5120]{1,0:T(8,128)(2,1)} %get-tuple-element.32), channel_id=1, source_target_pairs={{0,3},{4,7},{8,11},{12,15},{16,19},{20,23},{24,27},{28,31},{1,0},{... | collective-permute-start | bytes 983048 | tf_op jit(solution)/shard_map/ppermute | solution.py:417
  57.7 6.7 %collective-permute-done.13.second = bf16[32,5120]{1,0:T(8,128)(2,1)S(1)} collective-permute-done((bf16[32,5120]{1,0:T(8,128)(2,1)S(1)}, bf16[32,5120]{1,0:T(8,128)(2,1)S(1)}, u32[]{:S(2)}, u32[]{:S(2)}) %collective-permute-start.13) | collective-permute-done | bytes 327712 | tf_op jit(solution)/shard_map/ppermute | solution.py:416
  64.4 0.8 add.16
  65.2 2.9 %collective-permute-start.14 = (bf16[32,5120]{1,0:T(8,128)(2,1)}, bf16[32,5120]{1,0:T(8,128)(2,1)}, u32[]{:S(2)}, u32[]{:S(2)}) collective-permute-start(bf16[32,5120]{1,0:T(8,128)(2,1)} %add.16), channel_id=1, source_target_pairs={{0,35},{4,39},{8,43},{12,47},{16,51},{20,55},{24,59},{28,63},{1,32... | collective-permute-start | bytes 983048 | tf_op jit(solution)/shard_map/ppermute | solution.py:419
  68.1 1.7 %copy.14.weight = bf16[5120,64]{1,0:T(8,128)(2,1)S(1)} copy(bf16[5120,64]{0,1:T(8,128)(2,1)} %param.25) | data formatting | bytes 1310720 | tf_op args[12]
  69.8 0.0 collective-permute-done.12.p1
  69.8 4.0 %collective-permute-done.14.p2 = bf16[32,5120]{1,0:T(8,128)(2,1)} collective-permute-done((bf16[32,5120]{1,0:T(8,128)(2,1)}, bf16[32,5120]{1,0:T(8,128)(2,1)}, u32[]{:S(2)}, u32[]{:S(2)}) %collective-permute-start.14) | collective-permute-done | bytes 327712 | tf_op jit(solution)/shard_map/ppermute | solution.py:419
  73.8 0.0 copy-done
  73.8 0.0 copy-done.1
  73.8 0.0 copy-done.2
  73.8 0.0 copy-done.3
  73.8 0.0 copy-done.4
  73.8 1.9 %head.1 = f32[32,64]{1,0:T(8,128)S(1)} custom-call(s32[4]{0:T(128)S(1)} %copy-done.2, f32[4]{0:T(128)S(1)} %copy-done.3, s32[32]{0:T(128)S(1)} %copy-done.4, bf16[32,5120]{1,0:T(8,128)(2,1)S(1)} %get-tuple-element.31.p0, bf16[32,5120]{1,0:T(8,128)(2,1)} %collective-permute-done.12.p1, bf16[32,5120]{1,0:T(8,128)(2,1)} %collective-permute-done.14.p2, ...), custom_call_target="tpu_custom_call" | custom-call | tf_op jit(solution)/shard_map/head/pallas_call | solution.py:367
  75.8 1.3 %collective-permute-start.15 = (f32[32,64]{1,0:T(8,128)S(1)}, f32[32,64]{1,0:T(8,128)S(1)}, u32[]{:S(2)}, u32[]{:S(2)}) collective-permute-start(f32[32,64]{1,0:T(8,128)S(1)} %head.1), channel_id=1, source_target_pairs={{0,128},{64,192},{128,0},{192,64},{1,129},{65,193},{129,1},{193,65... | collective-permute-start | bytes 24584 | tf_op jit(solution)/shard_map/ppermute | solution.py:423
  77.1 2.2 %collective-permute-start.16 = (f32[32,64]{1,0:T(8,128)S(1)}, f32[32,64]{1,0:T(8,128)S(1)}, u32[]{:S(2)}, u32[]{:S(2)}) collective-permute-start(f32[32,64]{1,0:T(8,128)S(1)} %head.1), channel_id=1, source_target_pairs={{0,64},{64,128},{128,192},{192,0},{1,65},{65,129},{129,193},{193,1... | collective-permute-start | bytes 24584 | tf_op jit(solution)/shard_map/ppermute | solution.py:423
  79.3 0.0 collective-permute-start.17
  79.3 1.8 %collective-permute-done.15 = f32[32,64]{1,0:T(8,128)S(1)} collective-permute-done((f32[32,64]{1,0:T(8,128)S(1)}, f32[32,64]{1,0:T(8,128)S(1)}, u32[]{:S(2)}, u32[]{:S(2)}) %collective-permute-start.15) | collective-permute-done | bytes 8224 | tf_op jit(solution)/shard_map/ppermute | solution.py:423
  81.1 0.0 collective-permute-done.16
  81.1 3.1 %collective-permute-done.17 = f32[32,64]{1,0:T(8,128)S(1)} collective-permute-done((f32[32,64]{1,0:T(8,128)S(1)}, f32[32,64]{1,0:T(8,128)S(1)}, u32[]{:S(2)}, u32[]{:S(2)}) %collective-permute-start.17) | collective-permute-done | bytes 8224 | tf_op jit(solution)/shard_map/ppermute | solution.py:423
  84.2 0.6 add_add_fusion
  (2 shorter events, 0.0 us)
Async XLA Ops:
  1.6 18.7 %collective-permute-start.5 = (bf16[1280,640]{1,0:T(8,128)(2,1)S(1)}, bf16[1280,640]{1,0:T(8,128)(2,1)S(1)}, u32[]{:S(2)}, u32[]{:S(2)}) collective-permute-start(bf16[1280,640]{1,0:T(8,128)(2,1)S(1)} %get-tuple-element.21.mine_pack), channel_id=1, source_target_pairs={{0,4},{4,0},{8,12},{12,8},{16,20},{20,16},{24,28},{28,24},{32,36},... | collective-permute-start | bytes 4915208 | tf_op jit(solution)/shard_map/ppermute | solution.py:396
  1.7 7.8 %collective-permute-start.1 = (bf16[128,640]{1,0:T(8,128)(2,1)S(1)}, bf16[128,640]{1,0:T(8,128)(2,1)S(1)}, u32[]{:S(2)}, u32[]{:S(2)}) collective-permute-start(bf16[128,640]{1,0:T(8,128)(2,1)S(1)} %get-tuple-element.20.second), channel_id=1, source_target_pairs={{0,8},{4,12},{8,16},{12,20},{16,24},{20,28},{24,0},{28,4},{32,40},... | collective-permute-start | bytes 491528 | tf_op jit(solution)/shard_map/ppermute | solution.py:399
  3.3 6.5 %collective-permute-start = (bf16[128,640]{1,0:T(8,128)(2,1)S(1)}, bf16[128,640]{1,0:T(8,128)(2,1)S(1)}, u32[]{:S(2)}, u32[]{:S(2)}) collective-permute-start(bf16[128,640]{1,0:T(8,128)(2,1)S(1)} %get-tuple-element.20.second), channel_id=1, source_target_pairs={{0,32},{4,36},{8,40},{12,44},{16,48},{20,52},{24,56},{28,60},{32,0... | collective-permute-start | bytes 491528 | tf_op jit(solution)/shard_map/ppermute | solution.py:397
  5.2 6.0 %collective-permute-start.2 = (bf16[128,640]{1,0:T(8,128)(2,1)S(1)}, bf16[128,640]{1,0:T(8,128)(2,1)S(1)}, u32[]{:S(2)}, u32[]{:S(2)}) collective-permute-start(bf16[128,640]{1,0:T(8,128)(2,1)S(1)} %get-tuple-element.20.second), channel_id=1, source_target_pairs={{0,24},{4,28},{8,0},{12,4},{16,8},{20,12},{24,16},{28,20},{32,56},... | collective-permute-start | bytes 491528 | tf_op jit(solution)/shard_map/ppermute | solution.py:399
  9.5 10.7 %collective-permute-start.9 = (bf16[128,640]{1,0:T(8,128)(2,1)S(1)}, bf16[128,640]{1,0:T(8,128)(2,1)S(1)}, u32[]{:S(2)}, u32[]{:S(2)}) collective-permute-start(bf16[128,640]{1,0:T(8,128)(2,1)S(1)} %collective-permute-done.1.rest_0_.first), channel_id=1, source_target_pairs={{0,8},{4,12},{8,16},{12,20},{16,24},{20,28},{24,0},{28,4},{32,40},... | collective-permute-start | bytes 491528 | tf_op jit(solution)/shard_map/ppermute | solution.py:402
  11.2 11.7 %collective-permute-start.8 = (bf16[128,640]{1,0:T(8,128)(2,1)S(1)}, bf16[128,640]{1,0:T(8,128)(2,1)S(1)}, u32[]{:S(2)}, u32[]{:S(2)}) collective-permute-start(bf16[128,640]{1,0:T(8,128)(2,1)S(1)} %hold.1), channel_id=1, source_target_pairs={{0,16},{4,20},{8,24},{12,28},{16,0},{20,4},{24,8},{28,12},{32,48},... | collective-permute-start | bytes 491528 | tf_op jit(solution)/shard_map/ppermute | solution.py:403
  14.0 14.4 %collective-permute-start.3 = (bf16[128,640]{1,0:T(8,128)(2,1)S(1)}, bf16[128,640]{1,0:T(8,128)(2,1)S(1)}, u32[]{:S(2)}, u32[]{:S(2)}) collective-permute-start(bf16[128,640]{1,0:T(8,128)(2,1)S(1)} %hold.1), channel_id=1, source_target_pairs={{0,8},{4,12},{8,16},{12,20},{16,24},{20,28},{24,0},{28,4},{32,40},... | collective-permute-start | bytes 491528 | tf_op jit(solution)/shard_map/ppermute | solution.py:401
  15.1 13.3 %collective-permute-start.4 = (bf16[128,640]{1,0:T(8,128)(2,1)S(1)}, bf16[128,640]{1,0:T(8,128)(2,1)S(1)}, u32[]{:S(2)}, u32[]{:S(2)}) collective-permute-start(bf16[128,640]{1,0:T(8,128)(2,1)S(1)} %hold.1), channel_id=1, source_target_pairs={{0,24},{4,28},{8,0},{12,4},{16,8},{20,12},{24,16},{28,20},{32,56},... | collective-permute-start | bytes 491528 | tf_op jit(solution)/shard_map/ppermute | solution.py:401
  22.8 25.1 %slice-start = ((s8[6553600]{0:T(1024)(128)(4,1)}), s8[4194304]{0:T(1024)(128)(4,1)S(1)}, s32[]{:S(2)}) async-start(s8[6553600]{0:T(1024)(128)(4,1)} %bitcast.6), calls=%async_computation | async-start | bytes 8388608
  25.5 22.4 %slice-start.1 = ((s8[6553600]{0:T(1024)(128)(4,1)}), s8[2359296]{0:T(1024)(128)(4,1)S(1)}, s32[]{:S(2)}) async-start(s8[6553600]{0:T(1024)(128)(4,1)} %bitcast.6), calls=%async_computation.1 | async-start | bytes 4718592
  25.5 11.1 %collective-permute-start.10 = (bf16[1312,128]{1,0:T(8,128)(2,1)S(1)}, bf16[1312,128]{1,0:T(8,128)(2,1)S(1)}, u32[]{:S(2)}, u32[]{:S(2)}) collective-permute-start(bf16[1312,128]{1,0:T(8,128)(2,1)S(1)} %get-tuple-element.29), channel_id=1, source_target_pairs={{0,16},{4,20},{8,24},{12,28},{16,0},{20,4},{24,8},{28,12},{32,48},... | collective-permute-start | bytes 1007624 | tf_op jit(solution)/shard_map/ppermute | solution.py:411
  31.0 7.8 %collective-permute-start.6 = (bf16[1312,128]{1,0:T(8,128)(2,1)S(1)}, bf16[1312,128]{1,0:T(8,128)(2,1)S(1)}, u32[]{:S(2)}, u32[]{:S(2)}) collective-permute-start(bf16[1312,128]{1,0:T(8,128)(2,1)S(1)} %get-tuple-element.25), channel_id=1, source_target_pairs={{0,24},{4,28},{8,0},{12,4},{16,8},{20,12},{24,16},{28,20},{32,56},... | collective-permute-start | bytes 1007624 | tf_op jit(solution)/shard_map/ppermute | solution.py:409
  32.0 9.6 %collective-permute-start.7 = (bf16[1312,128]{1,0:T(8,128)(2,1)S(1)}, bf16[1312,128]{1,0:T(8,128)(2,1)S(1)}, u32[]{:S(2)}, u32[]{:S(2)}) collective-permute-start(bf16[1312,128]{1,0:T(8,128)(2,1)S(1)} %get-tuple-element.26), channel_id=1, source_target_pairs={{0,8},{4,12},{8,16},{12,20},{16,24},{20,28},{24,0},{28,4},{32,40},... | collective-permute-start | bytes 1007624 | tf_op jit(solution)/shard_map/ppermute | solution.py:410
  41.8 6.1 %collective-permute-start.11 = (bf16[656,128]{1,0:T(8,128)(2,1)S(1)}, bf16[656,128]{1,0:T(8,128)(2,1)S(1)}, u32[]{:S(2)}, u32[]{:S(2)}) collective-permute-start(bf16[656,128]{1,0:T(8,128)(2,1)S(1)} %merge.1), channel_id=1, source_target_pairs={{0,32},{4,36},{8,40},{12,44},{16,48},{20,52},{24,56},{28,60},{32,0... | collective-permute-start | bytes 503816 | tf_op jit(solution)/shard_map/ppermute | solution.py:414
  50.0 23.8 %copy-start = (f32[32,2,5120]{2,1,0:T(2,128)S(1)}, f32[32,2,5120]{2,1,0:T(2,128)}, u32[]{:S(2)}) copy-start(f32[32,2,5120]{2,1,0:T(2,128)} %table.1) | copy-start | bytes 3932164
  50.0 23.8 %copy-start.1 = (bf16[1,32,5120]{2,1,0:T(8,128)(2,1)S(1)}, bf16[1,32,5120]{2,1,0:T(8,128)(2,1)}, u32[]{:S(2)}) copy-start(bf16[1,32,5120]{2,1,0:T(8,128)(2,1)} %param.22) | copy-start | bytes 983044
  50.0 23.8 %copy-start.2 = (s32[4]{0:T(128)S(1)}, s32[4]{0:T(128)}, u32[]{:S(2)}) copy-start(s32[4]{0:T(128)} %group_branch.3) | copy-start | bytes 52
  50.0 23.8 %copy-start.3 = (f32[4]{0:T(128)S(1)}, f32[4]{0:T(128)}, u32[]{:S(2)}) copy-start(f32[4]{0:T(128)} %guidance_w.1) | copy-start | bytes 52
  50.0 23.8 %copy-start.4 = (s32[32]{0:T(128)S(1)}, s32[32]{0:T(128)}, u32[]{:S(2)}) copy-start(s32[32]{0:T(128)} %frame_level.1) | copy-start | bytes 388
  50.0 14.4 %collective-permute-start.13 = (bf16[32,5120]{1,0:T(8,128)(2,1)S(1)}, bf16[32,5120]{1,0:T(8,128)(2,1)S(1)}, u32[]{:S(2)}, u32[]{:S(2)}) collective-permute-start(bf16[32,5120]{1,0:T(8,128)(2,1)S(1)} %get-tuple-element.34), channel_id=1, source_target_pairs={{0,3},{4,7},{8,11},{12,15},{16,19},{20,23},{24,27},{28,31},{1,0},{... | collective-permute-start | bytes 983048 | tf_op jit(solution)/shard_map/ppermute | solution.py:416
  56.2 13.6 %collective-permute-start.12 = (bf16[32,5120]{1,0:T(8,128)(2,1)}, bf16[32,5120]{1,0:T(8,128)(2,1)}, u32[]{:S(2)}, u32[]{:S(2)}) collective-permute-start(bf16[32,5120]{1,0:T(8,128)(2,1)} %get-tuple-element.32), channel_id=1, source_target_pairs={{0,3},{4,7},{8,11},{12,15},{16,19},{20,23},{24,27},{28,31},{1,0},{... | collective-permute-start | bytes 983048 | tf_op jit(solution)/shard_map/ppermute | solution.py:417
  65.2 8.6 %collective-permute-start.14 = (bf16[32,5120]{1,0:T(8,128)(2,1)}, bf16[32,5120]{1,0:T(8,128)(2,1)}, u32[]{:S(2)}, u32[]{:S(2)}) collective-permute-start(bf16[32,5120]{1,0:T(8,128)(2,1)} %add.16), channel_id=1, source_target_pairs={{0,35},{4,39},{8,43},{12,47},{16,51},{20,55},{24,59},{28,63},{1,32... | collective-permute-start | bytes 983048 | tf_op jit(solution)/shard_map/ppermute | solution.py:419
  75.8 5.3 %collective-permute-start.15 = (f32[32,64]{1,0:T(8,128)S(1)}, f32[32,64]{1,0:T(8,128)S(1)}, u32[]{:S(2)}, u32[]{:S(2)}) collective-permute-start(f32[32,64]{1,0:T(8,128)S(1)} %head.1), channel_id=1, source_target_pairs={{0,128},{64,192},{128,0},{192,64},{1,129},{65,193},{129,1},{193,65... | collective-permute-start | bytes 24584 | tf_op jit(solution)/shard_map/ppermute | solution.py:423
  77.1 4.0 %collective-permute-start.16 = (f32[32,64]{1,0:T(8,128)S(1)}, f32[32,64]{1,0:T(8,128)S(1)}, u32[]{:S(2)}, u32[]{:S(2)}) collective-permute-start(f32[32,64]{1,0:T(8,128)S(1)} %head.1), channel_id=1, source_target_pairs={{0,64},{64,128},{128,192},{192,0},{1,65},{65,129},{129,193},{193,1... | collective-permute-start | bytes 24584 | tf_op jit(solution)/shard_map/ppermute | solution.py:423
  79.3 4.9 %collective-permute-start.17 = (f32[32,64]{1,0:T(8,128)S(1)}, f32[32,64]{1,0:T(8,128)S(1)}, u32[]{:S(2)}, u32[]{:S(2)}) collective-permute-start(f32[32,64]{1,0:T(8,128)S(1)} %head.1), channel_id=1, source_target_pairs={{0,192},{64,0},{128,64},{192,128},{1,193},{65,1},{129,65},{193,129... | collective-permute-start | bytes 24584 | tf_op jit(solution)/shard_map/ppermute | solution.py:423
